TPU v7x, 32 devices: a whole 2x2x4 slice. The times are simulated.
32 devices in a mesh: dp: 8 (over z, y), tensor: 4 (over x, core).
Axes of the slice: x: 2, y: 2, z: 4, core: 2. Of those that a mesh axis runs over, the one named last changes fastest.
Arguments:
- word_vectors: bfloat16 [16384, 768], P(('dp', 'tensor')), may hold values from -6 to 6
- position_table: bfloat16 [512, 768], P(('dp', 'tensor')), may hold values from -3 to 3
- horizontal_table: bfloat16 [1024, 768], P(('dp', 'tensor')), may hold values from -3 to 3
- vertical_table: bfloat16 [1024, 768], P(('dp', 'tensor')), may hold values from -3 to 3
- height_table: bfloat16 [1024, 768], P(('dp', 'tensor')), may hold values from -3 to 3
- width_table: bfloat16 [1024, 768], P(('dp', 'tensor')), may hold values from -3 to 3
- embed_gain: float32 [768], replicated, may hold values from 0.25 to 1.75
- embed_shift: float32 [768], replicated, may hold values from -3 to 3
- w_query: bfloat16 [768, 768], P('tensor'), may hold values from -0.21875 to 0.21875
- b_query: float32 [768], P('tensor'), may hold values from -3 to 3
- w_key: bfloat16 [768, 768], P('tensor'), may hold values from -0.21875 to 0.21875
- w_value: bfloat16 [768, 768], P('tensor'), may hold values from -0.21875 to 0.21875
- b_value: float32 [768], P('tensor'), may hold values from -3 to 3
- w_out: bfloat16 [768, 768], P('tensor'), may hold values from -1.25 to 1.25
- b_out: float32 [768], replicated, may hold values from -3 to 3
- attn_gain: float32 [768], replicated, may hold values from 0.25 to 1.75
- attn_shift: float32 [768], replicated, may hold values from -3 to 3
- w_in: bfloat16 [768, 3072], P(None, 'tensor'), may hold values from -0.21875 to 0.21875
- b_in: float32 [3072], P('tensor'), may hold values from -3 to 3
- w_down: bfloat16 [3072, 768], P('tensor'), may hold values from -0.109375 to 0.109375
- b_down: float32 [768], replicated, may hold values from -3 to 3
- ffn_gain: float32 [768], replicated, may hold values from 0.25 to 1.75
- ffn_shift: float32 [768], replicated, may hold values from -3 to 3
- boxes: int32 [4, 16384], P(None, ('dp', 'tensor')), may hold values from 0 to 1023
- segments: int32 [32, 512], P('dp'), may hold values from 0 to 7, never falling along the last dimension, each value on 1 to 128 neighbouring positions
- offsets: int32 [32, 8], P('dp'), may hold values from 0 to 384
- cotangent: float32 [16384, 768], P(('dp', 'tensor')), may hold values from -6 to 6
Outputs:
- layer_out: float32 [16384, 768], P(('dp', 'tensor'))
- grad_word: float32 [16384, 768], P(('dp', 'tensor'))
- grad_position_table: float32 [512, 768], P(('dp', 'tensor'))
- grad_horizontal_table: float32 [1024, 768], P(('dp', 'tensor'))
- grad_vertical_table: float32 [1024, 768], P(('dp', 'tensor'))
- grad_height_table: float32 [1024, 768], P(('dp', 'tensor'))
- grad_width_table: float32 [1024, 768], P(('dp', 'tensor'))
- grad_embed_gain: float32 [768], replicated
- grad_embed_shift: float32 [768], replicated
- grad_w_query: float32 [768, 768], P('tensor')
- grad_b_query: float32 [768], P('tensor')
- grad_w_key: float32 [768, 768], P('tensor')
- grad_w_value: float32 [768, 768], P('tensor')
- grad_b_value: float32 [768], P('tensor')
- grad_w_out: float32 [768, 768], P('tensor')
- grad_b_out: float32 [768], replicated
- grad_attn_gain: float32 [768], replicated
- grad_attn_shift: float32 [768], replicated
- grad_w_in: float32 [768, 3072], P(None, 'tensor')
- grad_b_in: float32 [3072], P('tensor')
- grad_w_down: float32 [3072, 768], P('tensor')
- grad_b_down: float32 [768], replicated
- grad_ffn_gain: float32 [768], replicated
- grad_ffn_shift: float32 [768], replicated
Inputs may be any that keep to these rules, and one draw needn't show every extreme that they name: `segments`: in each sequence page ids start at 0 and never fall; each of the 8 pages holds 1 to 128 tokens.
All inputs are finite; a program needn't handle non-finite values.
Results may differ from a plain program's by a relative error of at most 0.014.
Values may be sent and summed in bfloat16 or wider, within the bound.
A program may use at most 128 MiB of HBM per device.

v0:
```python
import functools

import jax
import jax.numpy as jnp
from jax import lax
from jax.experimental import pallas as pl
from jax.experimental.pallas import tpu as pltpu
from jax.sharding import PartitionSpec as P

HEAD = 64
MESH = pl.DeviceIdType.MESH
BF16 = jnp.bfloat16
F32 = jnp.float32

epsilon = 1e-06
masked_score = -1e30


class Place:
    def __init__(self, bits):
        self.bits = bits
        self.dp = lax.axis_index("dp")
        self.t = lax.axis_index("tensor")
        self.core = self.t % 2
        self.half = self.t // 2

    def bit(self, i):
        return (self.dp // 2**i) % 2

    def dp_flip(self, mask):
        dp = self.dp
        for i in range(self.bits):
            if mask & (1 << i):
                dp = dp + 2**i - 2 * 2**i * self.bit(i)
        return dp

    def t_flip(self, mask):
        t = self.t
        if mask & 1:
            t = t + 1 - 2 * self.core
        if mask & 2:
            t = t + 2 - 4 * self.half
        return t

    def partner(self, way):
        if way == "core":
            return (self.dp, self.t_flip(1))
        if way == "half":
            return (self.dp, self.t_flip(2))
        return (self.dp_flip(1 << way), self.t)

    def greet(self):
        barrier = pltpu.get_barrier_semaphore()
        ways = ["core", "half"] + list(range(self.bits))
        for way in ways:
            pl.semaphore_signal(
                barrier, inc=1, device_id=self.partner(way), device_id_type=MESH
            )
        pl.semaphore_wait(barrier, len(ways))


class Links:
    def __init__(self, place, send_sems):
        self.place = place
        self.send_sems = send_sems
        self.sent = []
        self.count = 0

    def send(self, way, src, dst, recv_sem):
        copy = pltpu.make_async_remote_copy(
            src_ref=src,
            dst_ref=dst,
            send_sem=self.send_sems.at[self.count],
            recv_sem=recv_sem,
            device_id=self.place.partner(way),
            device_id_type=MESH,
        )
        copy.start()
        self.count += 1
        self.sent.append(copy)
        return copy

    def arrived(self, way, dst, recv_sem):
        pltpu.make_async_remote_copy(
            src_ref=dst,
            dst_ref=dst,
            send_sem=recv_sem,
            recv_sem=recv_sem,
            device_id=self.place.partner(way),
            device_id_type=MESH,
        ).wait_recv()

    def finish(self):
        for copy in self.sent:
            copy.wait_send()


def interleave(*steps):
    live = list(steps)
    while live:
        for step in list(live):
            try:
                next(step)
            except StopIteration:
                live.remove(step)


def tables_gather(place, links, own, full, sems):
    bits = place.bits
    line_masks = [2 * k for k in range(2 ** (bits - 1))]
    line_sem, half_sem, row_sem, cross_sem, core_sem = sems

    def at(dp_mask, t_mask):
        return full.at[place.dp_flip(dp_mask) * 4 + place.t_flip(t_mask)]

    def to_core(slab, key):
        links.send("core", slab, slab, core_sem.at[key])

    def onward(mask, slab_source, below):
        for b in range(below - 1, 0, -1):
            links.send(b, slab_source, at(mask, 0), line_sem.at[(mask | (1 << b)) // 2])
        links.send("half", slab_source, at(mask, 0), half_sem.at[mask // 2])
        links.send(0, slab_source, at(mask, 0), row_sem.at[mask // 2])
        links.send("core", slab_source, at(mask, 0), core_sem.at[mask * 2])

    onward(0, own, bits)
    yield
    order = []
    held = [0]
    for b in range(bits - 1, 0, -1):
        fresh = [m | (1 << b) for m in held]
        for m in fresh:
            order.append((m, b))
        held = held + fresh
    for mask, b in order:
        links.arrived(b, at(mask, 0), line_sem.at[mask // 2])
        onward(mask, at(mask, 0), b)
        yield
    low = place.bit(1)
    for pair in range(len(line_masks) // 2):
        base = 4 * pair
        for mask in (base, base + 2):
            links.arrived("half", at(mask, 2), half_sem.at[mask // 2])
            to_core(at(mask, 2), mask * 2 + 1)
            links.arrived(0, at(mask + 1, 0), row_sem.at[mask // 2])
            to_core(at(mask + 1, 0), (mask + 1) * 2)
        yield
        dp_other = place.dp_flip(base)
        clear = dp_other - 2 * low
        here_clear = clear * 4 + place.t_flip(2)
        links.send(0, full.at[here_clear], full.at[here_clear], cross_sem.at[2 * pair + low])
        row_dp = place.dp_flip(base + 1)
        raised = row_dp + 2 * (1 - low)
        here_raised = raised * 4 + place.t
        links.send(
            "half", full.at[here_raised], full.at[here_raised], cross_sem.at[2 * pair + 1 - low]
        )
        yield
    def core_arrivals(row):
        for mask in line_masks:
            for t_mask in (0, 2):
                links.arrived(
                    "core",
                    at(mask + row, t_mask + 1),
                    core_sem.at[(mask + row) * 2 + t_mask // 2],
                )

    core_arrivals(0)
    yield "near"
    for pair in range(len(line_masks) // 2):
        base = 4 * pair
        dp_cross = place.dp_flip(base + 1)
        clear = (dp_cross - 2 * low) * 4 + place.t_flip(2)
        links.arrived(0, full.at[clear], cross_sem.at[2 * pair + low])
        links.send("core", full.at[clear], full.at[clear], core_sem.at[(base + 2 * low + 1) * 2 + 1])
        raised = (dp_cross + 2 * (1 - low)) * 4 + place.t_flip(2)
        links.arrived("half", full.at[raised], cross_sem.at[2 * pair + 1 - low])
        links.send(
            "core", full.at[raised], full.at[raised], core_sem.at[(base + 2 * (1 - low) + 1) * 2 + 1]
        )
        yield
    core_arrivals(1)
    yield


def added(left, right):
    return (left.astype(F32) + right.astype(F32)).astype(BF16)


def product(left, right):
    return jnp.dot(left, right, preferred_element_type=F32)


def inner_rows(left, right):
    return lax.dot_general(left, right, (((0,), (0,)), ((), ())), preferred_element_type=F32)


def against_rows(left, right):
    return lax.dot_general(left, right, (((1,), (1,)), ((), ())), preferred_element_type=F32)


CHUNKS = 2


def chunk_rows(place, weights, j, near):
    side = weights.shape[2] // 2
    rows = side // CHUNKS
    row_bit = place.bit(0) if near else 1 - place.bit(0)
    start = row_bit * side + (j % CHUNKS) * rows
    return j // CHUNKS, pl.ds(pl.multiple_of(start, rows), rows)


class Weights:
    def __init__(self, place, weights, send_sems, recv_sems, own_send, own_recv):
        self.place = place
        self.weights = weights
        self.send_sems = send_sems
        self.recv_sems = recv_sems
        self.own_send = own_send
        self.own_recv = own_recv

    def copy(self, way, lane, j, t, near, to=None):
        matrix, rows = chunk_rows(self.place, self.weights, j, near)
        block = self.weights.at[matrix, t, rows]
        return pltpu.make_async_remote_copy(
            src_ref=block,
            dst_ref=block,
            send_sem=self.send_sems.at[lane, j],
            recv_sem=self.recv_sems.at[lane, j],
            device_id=self.place.partner(way),
            device_id_type=MESH,
        )

    def own(self, i):
        block = self.weights.at[i, self.place.t]
        return pltpu.make_async_remote_copy(
            src_ref=block,
            dst_ref=block,
            send_sem=self.own_send.at[i],
            recv_sem=self.own_recv.at[i],
            device_id=self.place.partner("core"),
            device_id_type=MESH,
        )

    def own_arrived(self, i):
        block = self.weights.at[i, self.place.t_flip(1)]
        pltpu.make_async_remote_copy(
            src_ref=block,
            dst_ref=block,
            send_sem=self.own_send.at[i],
            recv_sem=self.own_recv.at[i],
            device_id=self.place.partner("core"),
            device_id_type=MESH,
        ).wait_recv()

    def issue(self, j):
        self.copy("half", 0, j, self.place.t, True).start()

    def take_half(self, j):
        other = self.place.t_flip(2)
        self.copy("half", 0, j, other, True).wait_recv()
        self.copy(0, 1, j, other, True).start()
        self.copy("core", 2, j, other, True).start()

    def take_row(self, j):
        other = self.place.t_flip(2)
        self.copy(0, 1, j, other, False).wait_recv()
        self.copy("core", 3, j, other, False).start()

    def settle(self, j):
        cross = self.place.t_flip(3)
        self.copy("core", 2, j, cross, True).wait_recv()
        self.copy("core", 3, j, cross, False).wait_recv()

    def finish(self, count):
        for i in range(3):
            self.own(i).wait_send()

        def one(j, carry):
            self.copy("half", 0, j, self.place.t, True).wait_send()
            self.copy(0, 1, j, self.place.t_flip(2), True).wait_send()
            self.copy("core", 2, j, self.place.t_flip(2), True).wait_send()
            self.copy("core", 3, j, self.place.t_flip(2), False).wait_send()
            return carry

        lax.fori_loop(0, count, one, 0)


def row_counts(lookup_rows, device, owns, slab_rows, tokens):
    by_table = ((0, (0,)), (1, (1, 3)), (2, (2, 4)), (3, (5,)), (4, (6,)))
    if all(own % 16 == 0 for own in owns):
        pieces = []
        for k, which in by_table:
            at = lax.broadcasted_iota(jnp.int32, (owns[k], tokens), 0) + device * owns[k]
            piece = sum(jnp.where(at == lookup_rows[w], 1.0, 0.0) for w in which)
            pieces.append(piece.astype(BF16))
        spare = slab_rows - sum(owns)
        if spare:
            pieces.append(jnp.zeros((spare, tokens), BF16))
        return jnp.concatenate(pieces, axis=0)
    at = lax.broadcasted_iota(jnp.int32, (slab_rows, tokens), 0)
    total = jnp.zeros((slab_rows, tokens), F32)
    first = 0
    for k, which in by_table:
        for w in which:
            local = lookup_rows[w] - device * owns[k]
            inside = (local >= 0) & (local < owns[k])
            total = total + jnp.where(at == jnp.where(inside, local + first, -1), 1.0, 0.0)
        first += owns[k]
    return total.astype(BF16)


def lookup_rows_of(boxes, segments, offsets, t):
    tokens = segments.shape[1]
    pages = offsets.shape[1]
    seg = segments[pl.ds(t, 1), :]
    label = lax.broadcasted_iota(jnp.int32, (pages, tokens), 0)
    place_in = lax.broadcasted_iota(jnp.int32, (pages, tokens), 1).astype(F32)
    member = label == seg
    starts = jnp.min(jnp.where(member, place_in, float(tokens)), axis=1, keepdims=True)
    shift_row = offsets[pl.ds(t, 1), :].astype(F32)
    eye = lax.broadcasted_iota(jnp.int32, (pages, pages), 0) == lax.broadcasted_iota(
        jnp.int32, (pages, pages), 1
    )
    shift = jnp.sum(jnp.where(eye, shift_row, 0.0), axis=1, keepdims=True)
    moved = jnp.sum(jnp.where(member, place_in - starts + shift, 0.0), axis=0, keepdims=True)
    positions = moved.astype(jnp.int32)
    x0, y0, x1, y1 = (boxes[i : i + 1, :] for i in range(4))
    return (positions, x0, y0, x1, y1, jnp.abs(y1 - y0), jnp.abs(x1 - x0)), seg


def norm_parts(values):
    width = values.shape[1]
    row_mean = jnp.sum(values, axis=1, keepdims=True) * (1.0 / width)
    row_var = jnp.sum(values * values, axis=1, keepdims=True) * (1.0 / width) - row_mean * row_mean
    scaled = lax.rsqrt(row_var + epsilon)
    return (values - row_mean) * scaled, scaled


ROWS = 64


def by_rows(count, step):
    def one(i, carry):
        step(pl.ds(pl.multiple_of(i * ROWS, ROWS), ROWS))
        return carry

    lax.fori_loop(0, count // ROWS, one, 0)


def head_blocks(tokens):
    half, reach = tokens // 2, 128
    return ((0, half, 0, half + reach), (half, half, half - reach, half + reach))


def mask_pages(segments_row, masks):
    tokens = segments_row.shape[1]
    rows = jnp.broadcast_to(segments_row.astype(F32), (8, tokens))
    columns = jnp.transpose(rows)
    for i, (q, nq, k, nk) in enumerate(head_blocks(tokens)):
        same = columns[k : k + nk, 0:1] == rows[0:1, q : q + nq]
        masks[i] = jnp.where(same, 0.0, masked_score).astype(masks.dtype)


def forward_kernel(
    bits,
    owns,
    slab,
    square,
    wide,
    tall,
    vectors,
    word,
    boxes,
    segments,
    offsets,
    cotangent,
    layer_out,
    grad_sum,
    grad_vectors,
    weights_out,
    inputs_low,
    centered_in,
    scaled_in,
    projected,
    mixed,
    stats,
    mid_low,
    centered_mid,
    scaled_mid,
    hidden,
    slopes,
    tables,
    counts,
    weights,
    biases,
    normed,
    total,
    masks,
    send_sems,
    line_sem,
    half_sem,
    row_sem,
    cross_sem,
    core_sem,
    weight_send,
    weight_recv,
    own_send,
    own_recv,
    bias_sems,
    local_sems,
):
    place = Place(bits)
    tokens, width = word.shape
    dps = 2**bits
    slab_rows = slab.shape[0]
    t = place.t
    place.greet()
    links = Links(place, send_sems)
    flow = Weights(place, weights, weight_send, weight_recv, own_send, own_recv)
    chunks = 3 * CHUNKS
    local = pltpu.make_async_copy(slab, tables.at[place.dp * 4 + t], local_sems.at[3])
    local.start()
    owned = [
        pltpu.make_async_copy(source, weights.at[i, t], local_sems.at[i])
        for i, source in enumerate((square, wide, tall))
    ]
    for copy in owned:
        copy.start()
    gather = tables_gather(
        place, links, slab, tables, (line_sem, half_sem, row_sem, cross_sem, core_sem)
    )
    next(gather)
    bias = vectors.at[pl.ds(8, 8)]
    biases[t] = vectors[8:16]
    links.send("core", bias, biases.at[t], bias_sems.at[0])
    links.send("half", bias, biases.at[t], bias_sems.at[1])
    for i, copy in enumerate(owned):
        copy.wait()
        flow.own(i).start()
    flow.issue(0)
    flow.issue(1)

    lookup, seg = lookup_rows_of(boxes, segments, offsets, t)

    def count_dp(dp, carry):
        for j in range(4):
            counts[dp, j * slab_rows : (j + 1) * slab_rows, :] = row_counts(
                lookup, dp * 4 + j, owns, slab_rows, tokens
            )
        return carry

    lax.fori_loop(0, dps, count_dp, 0)
    mask_pages(seg, masks)
    total[...] = word[...].astype(F32)
    local.wait()

    def embed(row_bit):
        def one(i, carry):
            dp = 2 * i + row_bit
            rows = tables[pl.ds(dp * 4, 4)].reshape(4 * slab_rows, width)
            total[...] += inner_rows(counts[dp], rows)
            return carry

        lax.fori_loop(0, dps // 2, one, 0)

    for step in gather:
        if step == "near":
            break
    links.arrived("half", biases.at[place.t_flip(2)], bias_sems.at[1])
    links.send("core", biases.at[place.t_flip(2)], biases.at[place.t_flip(2)], bias_sems.at[2])
    flow.take_half(0)
    flow.issue(2)
    embed(place.bit(0))
    flow.take_half(1)
    flow.issue(3)
    for step in gather:
        pass
    flow.take_row(0)
    embed(1 - place.bit(0))
    flow.take_row(1)

    def norm_in(rows):
        centered, scaled = norm_parts(total[rows])
        centered_in[rows] = centered.astype(BF16)
        scaled_in[rows] = scaled
        result = centered * vectors[0:1] + vectors[1:2]
        normed[rows] = result
        inputs_low[rows] = result.astype(BF16)

    by_rows(tokens, norm_in)
    links.arrived("core", biases.at[place.t_flip(1)], bias_sems.at[0])
    links.arrived("core", biases.at[place.t_flip(3)], bias_sems.at[2])
    flow.own_arrived(0)
    flow.settle(0)
    flow.settle(1)
    fourth = width // 4

    def project(j, carry):
        columns = jnp.transpose(biases[j])
        zeros = jnp.zeros((fourth, 1), F32)
        column = jnp.concatenate(
            [columns[0:fourth, 1:2], zeros, columns[fourth : 2 * fourth, 1:2]], axis=0
        )
        projected[j] = (
            against_rows(weights[0, j, : 3 * fourth, :], inputs_low[...]) + column
        ).astype(BF16)
        return carry

    lax.fori_loop(0, 4, project, 0)
    flow.take_half(2)
    flow.issue(4)

    def attend(j, carry):
        for h in range(fourth // HEAD):
            rows = slice(h * HEAD, (h + 1) * HEAD)
            key_rows = slice(fourth + h * HEAD, fourth + (h + 1) * HEAD)
            value_rows = slice(2 * fourth + h * HEAD, 2 * fourth + (h + 1) * HEAD)
            for i, (q, nq, k, nk) in enumerate(head_blocks(tokens)):
                scores = (
                    inner_rows(
                        projected[j, key_rows, k : k + nk], projected[j, rows, q : q + nq]
                    )
                    * HEAD ** (-0.5)
                    + masks[i]
                )
                peak = jnp.max(scores, axis=0, keepdims=True)
                exponent = jnp.exp(scores - peak)
                all_of = jnp.sum(exponent, axis=0, keepdims=True)
                stats[j, h : h + 1, q : q + nq] = peak + jnp.log(all_of)
                share = (exponent * (1.0 / all_of)).astype(BF16)
                mixed[j, rows, q : q + nq] = product(
                    projected[j, value_rows, k : k + nk], share
                ).astype(BF16)
        return carry

    def attend_and_pass(j, carry):
        attend(j, carry)

        @pl.when(j < 2)
        def _():
            flow.take_row(j + 2)

        @pl.when(j < 2)
        def _():
            flow.take_half(j + 3)

        @pl.when(j < 1)
        def _():
            flow.issue(j + 5)

        return carry

    lax.fori_loop(0, 4, attend_and_pass, 0)
    out_rows = weights[0, :, 3 * fourth :, :].reshape(width, width)
    total[...] = inner_rows(mixed[...].reshape(width, tokens), out_rows)
    flow.take_row(4)
    flow.take_half(5)

    def norm_mid(rows):
        centered, scaled = norm_parts(total[rows] + vectors[2:3] + normed[rows])
        centered_mid[rows] = centered.astype(BF16)
        scaled_mid[rows] = scaled
        result = centered * vectors[3:4] + vectors[4:5]
        normed[rows] = result
        mid_low[rows] = result.astype(BF16)

    by_rows(tokens, norm_mid)
    total[...] = jnp.zeros_like(total)
    columns = 256

    def feed(j):
        def one(n, carry):
            at = pl.ds(pl.multiple_of(n * columns, columns), columns)
            before = product(mid_low[...], weights[1, j, :, at]) + biases[j, 0:1, at]
            share = 0.5 * (1.0 + lax.erf(before * 0.5**0.5))
            hidden[j, :, at] = (before * share).astype(BF16)
            density = jnp.exp(before * before * -0.5) * 0.3989422804014327
            slopes[j, :, at] = (share + before * density).astype(BF16)
            return carry

        lax.fori_loop(0, width // columns, one, 0)
        total[...] += product(hidden[j], weights[2, j])

    flow.own_arrived(1)
    flow.own_arrived(2)

    def feed_near(i, carry):
        feed(t + i * (1 - 2 * place.core))
        return carry

    lax.fori_loop(0, 2, feed_near, 0)
    flow.take_row(5)
    for j in range(CHUNKS, chunks):
        flow.settle(j)
    out_copy = pltpu.make_async_copy(weights, weights_out, local_sems.at[0])
    out_copy.start()

    def feed_far(i, carry):
        feed(place.t_flip(2) + i * (1 - 2 * place.core))
        return carry

    lax.fori_loop(0, 2, feed_far, 0)
    grad_vectors[...] = jnp.zeros_like(grad_vectors)

    def norm_out(rows):
        centered, scaled = norm_parts(total[rows] + vectors[5:6] + normed[rows])
        layer_out[rows] = centered * vectors[6:7] + vectors[7:8]
        grad = cotangent[rows]
        grad_sum[rows] = norm_back(grad, centered, scaled, vectors[6:7])
        grad_vectors[0:1] += jnp.sum(grad * centered, axis=0, keepdims=True)
        grad_vectors[1:2] += jnp.sum(grad, axis=0, keepdims=True)
        grad_vectors[2:3] += jnp.sum(grad_sum[rows], axis=0, keepdims=True)

    by_rows(tokens, norm_out)
    out_copy.wait()
    links.finish()
    flow.finish(chunks)


def norm_back(grad_out, centered, scaled, norm_gain):
    width = grad_out.shape[1]
    grad_centered = grad_out * norm_gain
    first_mean = jnp.sum(grad_centered, axis=1, keepdims=True) * (1.0 / width)
    second_mean = jnp.sum(grad_centered * centered, axis=1, keepdims=True) * (1.0 / width)
    return scaled * (grad_centered - first_mean - centered * second_mean)


def forward_all(
    devices, owns, slab, square, wide, tall, vectors, word, boxes, segments, offsets, cotangent
):
    bits = (devices // 4).bit_length() - 1
    dps = 2**bits
    lines = 2 ** (bits - 1)
    tokens, width = word.shape
    anywhere = pl.BlockSpec(memory_space=pl.ANY)
    in_vmem = pl.BlockSpec(memory_space=pltpu.VMEM)
    slab_rows = slab.shape[0]
    fourth = width // 4
    shape = jax.ShapeDtypeStruct
    return pl.pallas_call(
        functools.partial(forward_kernel, bits, owns),
        out_shape=[
            shape((tokens, width), F32),
            shape((tokens, width), F32),
            shape((8, width), F32),
            shape((3, 4, width, width), BF16),
            shape((tokens, width), BF16),
            shape((tokens, width), BF16),
            shape((tokens, 1), F32),
            shape((4, 3 * fourth, tokens), BF16),
            shape((4, fourth, tokens), BF16),
            shape((4, 8, tokens), F32),
            shape((tokens, width), BF16),
            shape((tokens, width), BF16),
            shape((tokens, 1), F32),
            shape((4, tokens, width), BF16),
            shape((4, tokens, width), BF16),
        ],
        in_specs=[anywhere] * 4 + [in_vmem] * 6,
        out_specs=[in_vmem] * 3 + [anywhere] + [in_vmem] * 11,
        scratch_shapes=[
            pltpu.VMEM((devices, slab_rows, width), BF16),
            pltpu.VMEM((dps, 4 * slab_rows, tokens), BF16),
            pltpu.VMEM((3, 4, width, width), BF16),
            pltpu.VMEM((4, 8, width), F32),
            pltpu.VMEM((tokens, width), F32),
            pltpu.VMEM((tokens, width), F32),
            pltpu.VMEM((2, tokens // 2 + 128, tokens // 2), F32),
            pltpu.SemaphoreType.DMA((10 * lines + 40 + lines * bits,)),
            pltpu.SemaphoreType.DMA((lines,)),
            pltpu.SemaphoreType.DMA((lines,)),
            pltpu.SemaphoreType.DMA((lines,)),
            pltpu.SemaphoreType.DMA((lines,)),
            pltpu.SemaphoreType.DMA((4 * lines,)),
            pltpu.SemaphoreType.DMA((4, 3 * CHUNKS)),
            pltpu.SemaphoreType.DMA((4, 3 * CHUNKS)),
            pltpu.SemaphoreType.DMA((3,)),
            pltpu.SemaphoreType.DMA((3,)),
            pltpu.SemaphoreType.DMA((3,)),
            pltpu.SemaphoreType.DMA((4,)),
        ],
        name="forward_all",
        compiler_params=pltpu.CompilerParams(
            collective_id=0, has_side_effects=True, vmem_limit_bytes=60 * 2**20
        ),
    )(slab, square, wide, tall, vectors, word, boxes, segments, offsets, cotangent)


def ladder(rows, bits):
    left = [rows]
    for b in range(bits):
        halves = left[-1] % 32 == 0 and b < bits - 1
        left.append(left[-1] // 2 if halves else left[-1])
    return left


SLOTS = 3
PARTS = 3


class Sums:
    def __init__(self, place, outgoing, own, from_core, from_half, from_dp, total, sems, credit):
        self.place = place
        self.outgoing = outgoing
        self.own = own
        self.from_core = from_core
        self.from_half = from_half
        self.from_dp = from_dp
        self.total = total
        self.send_sems, self.recv_sems = sems
        self.credit = credit
        self.rows = own.shape[2]
        self.left = ladder(self.rows, place.bits)
        self.back = [b for b in range(place.bits) if self.left[b + 1] < self.left[b]]

    def copy(self, way, lane, j, src, dst):
        return pltpu.make_async_remote_copy(
            src_ref=src,
            dst_ref=dst,
            send_sem=self.send_sems.at[lane, j],
            recv_sem=self.recv_sems.at[lane, j],
            device_id=self.place.partner(way),
            device_id_type=MESH,
        )

    def start_of(self, level):
        start = 0
        for b in range(level):
            if self.left[b + 1] < self.left[b]:
                start = start + self.place.bit(b) * self.left[b + 1]
        return start

    def span(self, b, near):
        start, rows = self.start_of(b), self.left[b + 1]
        if rows < self.left[b]:
            bit = self.place.bit(b)
            start = start + (bit if near else 1 - bit) * rows
        return pl.ds(pl.multiple_of(start, 16), rows) if b or rows < self.left[0] else pl.ds(0, rows)

    def landing(self, b, j):
        first = sum(self.left[1 : b + 1])
        return self.from_dp.at[j, pl.ds(first, self.left[b + 1])]

    def core(self, j):
        slot = j % SLOTS
        return self.copy("core", 0, j, self.outgoing.at[slot], self.from_core.at[slot])

    def half(self, j):
        return self.copy("half", 1, j, self.own.at[j, 1], self.from_half.at[j])

    def dp(self, b, j):
        return self.copy(
            b, 2 + b, j, self.own.at[j, 0, self.span(b, False)], self.landing(b, j)
        )

    def gather(self, b, j, near=True):
        block = self.total.at[j, self.span(b, near)]
        return self.copy(b, 2 + self.place.bits + b, j, block, block)

    def launch(self, j):
        if j >= SLOTS:
            pl.semaphore_wait(self.credit, 1)
        self.core(j).start()

    def take_core(self, j, count):
        slot = j % SLOTS
        self.core(j).wait_recv()
        for which in (1, 0):
            self.own[j, which] = added(self.own[j, which], self.from_core[slot, which])
        if j + SLOTS < count:
            pl.semaphore_signal(
                self.credit, inc=1, device_id=self.place.partner("core"), device_id_type=MESH
            )

    def take_half(self, j):
        self.half(j).wait_recv()
        span = self.span(0, False)
        self.own[j, 0, span] = added(self.own[j, 0, span], self.from_half[j, span])
        self.dp(0, j).start()
        if self.left[1] < self.left[0]:
            span = self.span(0, True)
            self.own[j, 0, span] = added(self.own[j, 0, span], self.from_half[j, span])

    def take_dp(self, b, j):
        self.dp(b, j).wait_recv()
        span, first = self.span(b, True), sum(self.left[1 : b + 1])
        arrived = self.from_dp[j, pl.ds(first, self.left[b + 1])]
        if b == self.place.bits - 1:
            self.total[j, span] = added(self.own[j, 0, span], arrived)
            if self.back:
                self.gather(self.back[-1], j).start()
            return
        if self.left[b + 1] == self.left[b]:
            self.dp(b, j).wait_send()
        self.own[j, 0, span] = added(self.own[j, 0, span], arrived)
        self.dp(b + 1, j).start()

    def take_back(self, i, j):
        order = self.back[::-1]
        self.gather(order[i], j, False).wait_recv()
        if i + 1 < len(order):
            self.gather(order[i + 1], j).start()

    def stages(self):
        return 1 + self.place.bits + len(self.back)

    def stage(self, s, j):
        if s == 0:
            self.take_half(j)
        elif s <= self.place.bits:
            self.take_dp(s - 1, j)
        else:
            self.take_back(s - 1 - self.place.bits, j)

    def finish(self, count):
        for j in range(max(0, count - SLOTS), count):
            self.core(j).wait_send()

        def one(j, carry):
            self.half(j).wait_send()
            for b in range(self.place.bits):
                if self.left[b + 1] < self.left[b] or b == self.place.bits - 1:
                    self.dp(b, j).wait_send()
            for b in self.back:
                self.gather(b, j).wait_send()
            return carry

        lax.fori_loop(0, count, one, 0)


def table_reduce(place, links, slab_at, width_of, columns, order, halves, lines, half_sems, dp_sems):
    bits = place.bits

    def slab(mask, half):
        return slab_at(place.dp_flip(mask), half).at[:, columns]

    def add(mask, half, landed):
        target = slab(mask, half)
        target[...] = added(target[...], landed[...])

    def lowest(mask):
        return (mask & -mask).bit_length() - 1 if mask else bits

    mine, theirs = place.half, 1 - place.half
    masks = sorted(range(2**bits), key=lambda m: (lowest(m), m))
    slot = 0
    base = {}
    for b in range(bits):
        for h in range(2 if (b == 0 and order == "row") else 1):
            base[b, h] = slot
            slot += 2 ** (bits - 1 - b)

    def index(b, h, mask):
        return base[b, h] + (mask >> (b + 1))

    def send_dp(b, mask, half, h):
        i = index(b, h, mask ^ (1 << b))
        links.send(b, slab(mask, half), lines.at[i], dp_sems.at[i])

    def take_dp(b, mask, half, h):
        i = index(b, h, mask)
        links.arrived(b, lines.at[i], dp_sems.at[i])
        add(mask, half, lines.at[i])

    if order == "half":
        for mask in masks:
            links.send("half", slab(mask, theirs), halves.at[mask], half_sems.at[mask])
        yield
        for mask in masks:
            links.arrived("half", halves.at[mask], half_sems.at[mask])
            add(mask, mine, halves.at[mask])
            if mask & 1:
                send_dp(0, mask, mine, 0)
            yield
    else:
        for h, half in ((1, theirs), (0, mine)):
            for mask in masks:
                if mask & 1:
                    send_dp(0, mask, half, h)
        yield
        kept = [m for m in masks if not m & 1]
        for mask in kept:
            take_dp(0, mask, theirs, 1)
            links.send("half", slab(mask, theirs), halves.at[mask], half_sems.at[mask])
            yield
        for mask in kept:
            take_dp(0, mask, mine, 0)
            yield
        for mask in kept:
            links.arrived("half", halves.at[mask], half_sems.at[mask])
            add(mask, mine, halves.at[mask])
            if bits > 1 and mask & 2:
                send_dp(1, mask, mine, 0)
            yield
    for b in range(0 if order == "half" else 1, bits):
        for mask in masks:
            if mask % (2 << b):
                continue
            take_dp(b, mask, mine, 0)
            if b + 1 < bits and mask & (2 << b):
                send_dp(b + 1, mask, mine, 0)
            yield


def vector_reduce(place, links, vectors, landing, sems):
    for i, way in enumerate(["core", "half"] + list(range(place.bits))):
        links.send(way, vectors.at[i], landing.at[i], sems.at[i])
        yield
        links.arrived(way, landing.at[i], sems.at[i])
        vectors[i + 1] = vectors[i] + landing[i]


def backward_kernel(
    bits,
    owns,
    slab_rows,
    weights_in,
    vectors,
    boxes,
    segments,
    offsets,
    grad_sum,
    ffn_vectors,
    inputs_low,
    centered_in,
    scaled_in,
    projected,
    mixed,
    stats,
    mid_low,
    centered_mid,
    scaled_mid,
    hidden_in,
    slopes_in,
    grad_word,
    weight_sums,
    table_sum,
    vector_sum,
    held,
    hidden,
    slopes,
    outgoing,
    own,
    from_core,
    from_half,
    from_dp,
    halves,
    lines_half,
    lines_row,
    words,
    lookups,
    vector_terms,
    vector_land,
    total,
    low,
    masks,
    grad_heads,
    grad_projected,
    counts,
    send_sems,
    sum_send,
    sum_recv,
    half_sems,
    line_half_sems,
    line_row_sems,
    vector_sems,
    word_sems,
    local_sems,
    credit,
):
    place = Place(bits)
    tokens, width = grad_sum.shape
    dps = 2**bits
    t, core = place.t, place.core
    fourth = width // 4
    part = width // PARTS
    quarter_rows = width
    loads = {}
    for i, (matrix, slot) in enumerate(((2, 0), (1, 1), (0, 0))):
        loads[matrix] = [
            pltpu.make_async_copy(
                weights_in.at[matrix, q],
                held.at[pl.ds((slot * 4 + q) * quarter_rows, quarter_rows)],
                local_sems.at[matrix, q],
            )
            for q in range(4)
        ]
    early = [
        pltpu.make_async_copy(hidden_in, hidden, local_sems.at[3, 0]),
        pltpu.make_async_copy(slopes_in, slopes, local_sems.at[3, 1]),
    ]
    for copy in loads[2] + early + loads[1]:
        copy.start()
    place.greet()
    links = Links(place, send_sems)
    sums = Sums(
        place, outgoing, own, from_core, from_half, from_dp, weight_sums, (sum_send, sum_recv), credit
    )
    chunks = 3 * PARTS

    def quarter(parity, other):
        q = t + other * (2 - 4 * place.half)
        return q + 1 - 2 * core if parity else q

    def held_rows(slot, q, first=0, rows=width):
        start = (slot * 4 + q) * quarter_rows + first
        return held[pl.ds(pl.multiple_of(start, 16), rows)]

    lookup, seg = lookup_rows_of(boxes, segments, offsets, t)
    mask_pages(seg, masks)
    lookups[0] = jnp.concatenate(list(lookup) + [lookup[0]], axis=0)
    links.send("core", lookups.at[0], lookups.at[1], word_sems.at[0])

    def start_rows(rows):
        low[rows] = grad_sum[rows].astype(BF16)

    by_rows(tokens, start_rows)
    vector_terms[0] = jnp.zeros_like(vector_terms[0])
    vector_terms[0, 4:6] = ffn_vectors[0:2]
    vector_terms[0, 7:8] = ffn_vectors[2:3]
    for copy in loads[2] + early:
        copy.wait()

    def chunk(j, term):
        slot = j % SLOTS
        if j >= SLOTS:
            sums.core(j - SLOTS).wait_send()

        def out(i, carry):
            outgoing[slot, i] = term(quarter(1, i)).astype(BF16)
            return carry

        def keep(i, carry):
            own[j, i] = term(quarter(0, i)).astype(BF16)
            return carry

        lax.fori_loop(0, 2, out, 0)
        sums.launch(j)
        lax.fori_loop(0, 2, keep, 0)

    def down_term(part_at, q):
        at = pl.ds(part_at * part, part)
        back = against_rows(low[...], held_rows(0, q, part_at * part, part))
        before = (back * slopes[q, :, at].astype(F32)).astype(BF16)
        slopes[q, :, at] = before
        vector_terms[0, pl.ds(8 + q, 1), at] = jnp.sum(
            before.astype(F32), axis=0, keepdims=True
        )
        return inner_rows(hidden[q, :, at], low[...])

    for p in range(PARTS):
        chunk(p, functools.partial(down_term, p))
        if p:
            sums.take_core(p - 1, chunks)
            sums.half(p - 1).start()
    for copy in loads[0]:
        copy.start()
    sums.take_core(PARTS - 1, chunks)
    for copy in loads[1]:
        copy.wait()
    for p in range(PARTS):
        columns = slice(p * part, (p + 1) * part)
        chunk(PARTS + p, lambda q: inner_rows(mid_low[:, columns], slopes[q]))
        if p:
            sums.take_core(PARTS + p - 1, chunks)
    total[...] = grad_sum[...]

    def mid_term(q, carry):
        total[...] += against_rows(slopes[q], held_rows(1, q))
        return carry

    lax.fori_loop(0, 4, mid_term, 0)
    sums.take_core(2 * PARTS - 1, chunks)

    done = [0]
    stages = sums.stages()

    def tick(limit):
        k = done[0]
        done[0] += 1
        for s in range(stages):
            j = k - s
            if j < 0 or j >= limit:
                continue
            sums.stage(s, j)
            if s == 0 and j + 2 < limit:
                sums.half(j + 2).start()

    def mid_back(rows):
        centered = centered_mid[rows].astype(F32)
        grad = total[rows]
        result = norm_back(grad, centered, scaled_mid[rows], vectors[3:4])
        vector_terms[0, 2:3] += jnp.sum(grad * centered, axis=0, keepdims=True)
        vector_terms[0, 3:4] += jnp.sum(grad, axis=0, keepdims=True)
        vector_terms[0, 6:7] += jnp.sum(result, axis=0, keepdims=True)
        total[rows] = result
        low[rows] = result.astype(BF16)

    by_rows(tokens, mid_back)
    for copy in loads[0]:
        copy.wait()

    def out_back(q, carry):
        grad_heads[q] = against_rows(held_rows(0, q, 3 * fourth, fourth), low[...]).astype(BF16)
        return carry

    lax.fori_loop(0, 4, out_back, 0)
    scale = HEAD ** (-0.5)

    def attend_back(j, carry):
        for h in range(fourth // HEAD):
            rows = slice(h * HEAD, (h + 1) * HEAD)
            key_rows = slice(fourth + h * HEAD, fourth + (h + 1) * HEAD)
            value_rows = slice(2 * fourth + h * HEAD, 2 * fourth + (h + 1) * HEAD)
            grads = []
            for i, (q, nq, k, nk) in enumerate(head_blocks(tokens)):
                queries = projected[j, rows, q : q + nq]
                keys = projected[j, key_rows, k : k + nk]
                values = projected[j, value_rows, k : k + nk]
                grad = grad_heads[j, rows, q : q + nq]
                scores = inner_rows(keys, queries) * scale + masks[i].astype(F32)
                share = jnp.exp(scores - stats[j, h : h + 1, q : q + nq])
                back = inner_rows(values, grad)
                inner = jnp.sum(share * back, axis=0, keepdims=True)
                grad_scores = (share * (back - inner)).astype(BF16)
                grad_projected[j, rows, q : q + nq] = (product(keys, grad_scores) * scale).astype(BF16)
                grads.append(
                    (
                        against_rows(queries, grad_scores) * scale,
                        against_rows(grad, share.astype(BF16)),
                    )
                )
            reach = 128
            for target, (first, second) in zip((key_rows, value_rows), zip(*grads)):
                edge = tokens // 2 - reach
                joined = jnp.concatenate(
                    [
                        first[:, :edge],
                        first[:, edge:] + second[:, : 2 * reach],
                        second[:, 2 * reach :],
                    ],
                    axis=1,
                )
                grad_projected[j, target, :] = joined.astype(BF16)
        ones = jnp.ones((8, tokens), BF16)
        vector_terms[0, pl.ds(12 + j, 1), 0 : 3 * fourth] = against_rows(ones, grad_projected[j])[0:1]
        return carry

    for j in (0, 2):
        lax.fori_loop(j, j + 2, attend_back, 0)
        tick(chunks)

    def square_term(p, q):
        if p < PARTS - 1:
            return product(grad_projected[q, p * part : (p + 1) * part, :], inputs_low[...])
        return jnp.concatenate(
            [
                product(grad_projected[q, p * part :, :], inputs_low[...]),
                product(mixed[q], low[...]),
            ],
            axis=0,
        )

    for p in range(PARTS):
        chunk(2 * PARTS + p, functools.partial(square_term, p))

    def in_term(q, carry):
        total[...] += inner_rows(grad_projected[q], held_rows(0, q, 0, 3 * fourth))
        return carry

    lax.fori_loop(0, 4, in_term, 0)
    for p in range(PARTS):
        sums.take_core(2 * PARTS + p, chunks)

    def in_back(rows):
        centered = centered_in[rows].astype(F32)
        grad = total[rows]
        result = norm_back(grad, centered, scaled_in[rows], vectors[0:1])
        vector_terms[0, 0:1] += jnp.sum(grad * centered, axis=0, keepdims=True)
        vector_terms[0, 1:2] += jnp.sum(grad, axis=0, keepdims=True)
        total[rows] = result
        low[rows] = result.astype(BF16)

    by_rows(tokens, in_back)
    word_copy = pltpu.make_async_copy(total, grad_word, local_sems.at[3, 2])
    word_copy.start()
    links.send("core", low, words, word_sems.at[1])
    links.arrived("core", lookups.at[1], word_sems.at[0])
    tick(chunks)
    links.arrived("core", words, word_sems.at[1])

    def slab_at(dp, half):
        start = (dp * 2 + half) * slab_rows
        return held.at[pl.ds(pl.multiple_of(start, 16), slab_rows)]

    def table_term(dp, carry):
        for i in range(2):
            rows = tuple(lookups[i, w : w + 1, :] for w in range(7))
            for h in range(2):
                counts[i, h * slab_rows : (h + 1) * slab_rows, :] = row_counts(
                    rows, dp * 4 + h * 2 + core, owns, slab_rows, tokens
                )
        start = pl.multiple_of(dp * 2 * slab_rows, 16)
        held[pl.ds(start, 2 * slab_rows)] = (
            product(counts[0], low[...]) + product(counts[1], words[...])
        ).astype(BF16)
        return carry

    lax.fori_loop(0, dps, table_term, 0)
    split = width // 2
    steps = [
        table_reduce(
            place, links, slab_at, width, pl.ds(0, split), "half",
            halves.at[0], lines_half, half_sems.at[0], line_half_sems,
        ),
        table_reduce(
            place, links, slab_at, width, pl.ds(split, split), "row",
            halves.at[1], lines_row, half_sems.at[1], line_row_sems,
        ),
        vector_reduce(place, links, vector_terms, vector_land, vector_sems),
    ]

    def ticks():
        while done[0] < chunks + stages - 1:
            tick(chunks)
            yield
            yield
            yield

    interleave(ticks(), *steps)
    table_sum[...] = slab_at(place.dp, place.half)[...]
    vector_sum[...] = vector_terms[bits + 2]
    word_copy.wait()
    links.finish()
    sums.finish(chunks)


def backward_all(devices, owns, slab_rows, weights, vectors, boxes, segments, offsets, kept):
    bits = (devices // 4).bit_length() - 1
    dps = 2**bits
    tokens, width = kept[0].shape
    anywhere = pl.BlockSpec(memory_space=pl.ANY)
    in_vmem = pl.BlockSpec(memory_space=pltpu.VMEM)
    fourth, part = width // 4, width // PARTS
    chunks = 3 * PARTS
    landing = sum(ladder(part, bits)[1:])
    half_lines = dps - 1
    row_lines = dps - 1 + dps // 2
    held_rows = max(8 * width, 2 * dps * slab_rows)
    shape = jax.ShapeDtypeStruct
    return pl.pallas_call(
        functools.partial(backward_kernel, bits, owns, slab_rows),
        out_shape=[
            shape((tokens, width), F32),
            shape((chunks, part, width), BF16),
            shape((slab_rows, width), BF16),
            shape((16, width), F32),
        ],
        in_specs=[anywhere] + [in_vmem] * (2 + len(kept)) + [anywhere] * 2,
        out_specs=[anywhere] + [in_vmem] * 3,
        scratch_shapes=[
            pltpu.VMEM((held_rows, width), BF16),
            pltpu.VMEM((4, tokens, width), BF16),
            pltpu.VMEM((4, tokens, width), BF16),
            pltpu.VMEM((SLOTS, 2, part, width), BF16),
            pltpu.VMEM((chunks, 2, part, width), BF16),
            pltpu.VMEM((SLOTS, 2, part, width), BF16),
            pltpu.VMEM((chunks, part, width), BF16),
            pltpu.VMEM((chunks, landing, width), BF16),
            pltpu.VMEM((2, dps, slab_rows, width // 2), BF16),
            pltpu.VMEM((half_lines, slab_rows, width // 2), BF16),
            pltpu.VMEM((row_lines, slab_rows, width // 2), BF16),
            pltpu.VMEM((tokens, width), BF16),
            pltpu.VMEM((2, 8, tokens), jnp.int32),
            pltpu.VMEM((bits + 3, 16, width), F32),
            pltpu.VMEM((bits + 2, 16, width), F32),
            pltpu.VMEM((tokens, width), F32),
            pltpu.VMEM((tokens, width), BF16),
            pltpu.VMEM((2, tokens // 2 + 128, tokens // 2), BF16),
            pltpu.VMEM((4, fourth, tokens), BF16),
            pltpu.VMEM((4, 3 * fourth, tokens), BF16),
            pltpu.VMEM((2, 2 * slab_rows, tokens), BF16),
            pltpu.SemaphoreType.DMA((6 * dps + 40,)),
            pltpu.SemaphoreType.DMA((2 + 2 * bits, chunks)),
            pltpu.SemaphoreType.DMA((2 + 2 * bits, chunks)),
            pltpu.SemaphoreType.DMA((2, dps)),
            pltpu.SemaphoreType.DMA((half_lines,)),
            pltpu.SemaphoreType.DMA((row_lines,)),
            pltpu.SemaphoreType.DMA((bits + 2,)),
            pltpu.SemaphoreType.DMA((2,)),
            pltpu.SemaphoreType.DMA((4, 4)),
            pltpu.SemaphoreType.REGULAR,
        ],
        name="backward_all",
        compiler_params=pltpu.CompilerParams(
            collective_id=1, has_side_effects=True, vmem_limit_bytes=60 * 2**20
        ),
    )(weights, vectors, boxes, segments, offsets, *kept)


def body(
    devices,
    word_vectors,
    position_table,
    horizontal_table,
    vertical_table,
    height_table,
    width_table,
    embed_gain,
    embed_shift,
    w_query,
    b_query,
    w_key,
    w_value,
    b_value,
    w_out,
    b_out,
    attn_gain,
    attn_shift,
    w_in,
    b_in,
    w_down,
    b_down,
    ffn_gain,
    ffn_shift,
    boxes,
    segments,
    offsets,
    cotangent,
):
    own_rows, width = word_vectors.shape
    t = lax.axis_index("tensor")
    owned = (position_table, horizontal_table, vertical_table, height_table, width_table)
    slab_rows = sum(table.shape[0] for table in owned)
    slab_padded = -(-slab_rows // 16) * 16
    slab = jnp.concatenate(owned, axis=0)
    slab = jnp.pad(slab, ((0, slab_padded - slab_rows), (0, 0)))
    square = jnp.concatenate((w_query, w_key, w_value, w_out), axis=0)
    fourth = w_query.shape[0]
    bias_rows = jnp.concatenate([b_query, b_value, jnp.zeros((2 * fourth,), F32)])
    vectors = jnp.stack(
        [embed_gain, embed_shift, b_out, attn_gain, attn_shift, b_down, ffn_gain, ffn_shift]
        + [b_in, bias_rows]
        + [jnp.zeros_like(b_in)] * 6
    )
    owns = tuple(table.shape[0] for table in owned)
    layer_out, grad_ffn_sum, ffn_vectors, weights, *kept = forward_all(
        devices,
        owns,
        slab,
        square,
        w_in,
        w_down,
        vectors,
        word_vectors,
        boxes,
        segments,
        offsets,
        cotangent,
    )
    grad_word, weight_sums, table_sum, vector_sum = backward_all(
        devices,
        owns,
        slab_padded,
        weights,
        vectors,
        boxes,
        segments,
        offsets,
        (grad_ffn_sum, ffn_vectors, *kept),
    )
    tall_sum, wide_sum, square_sum = weight_sums.astype(F32).reshape(3, width, width)
    table_sum = table_sum.astype(F32)
    first = [0]
    for own in owns:
        first.append(first[-1] + own)
    bias_in = lax.dynamic_slice_in_dim(vector_sum, 8 + t, 1)[0]
    bias_row = lax.dynamic_slice_in_dim(vector_sum, 12 + t, 1)[0]
    bias_query, bias_value = bias_row[:fourth], bias_row[2 * fourth : 3 * fourth]
    return (
        layer_out,
        grad_word,
        *(table_sum[first[k] : first[k + 1]] for k in range(5)),
        vector_sum[0],
        vector_sum[1],
        square_sum[:fourth],
        bias_query,
        square_sum[fourth : 2 * fourth],
        square_sum[2 * fourth : 3 * fourth],
        bias_value,
        square_sum[3 * fourth :],
        vector_sum[6],
        vector_sum[2],
        vector_sum[3],
        wide_sum,
        bias_in,
        tall_sum,
        vector_sum[7],
        vector_sum[4],
        vector_sum[5],
    )


def solution(mesh):
    devices = mesh.shape["dp"] * mesh.shape["tensor"]
    both = P(("dp", "tensor"), None)
    rows = P("tensor", None)
    return jax.shard_map(
        functools.partial(body, devices),
        mesh=mesh,
        in_specs=(
            *(both,) * 6,
            P(),
            P(),
            rows,
            P("tensor"),
            rows,
            rows,
            P("tensor"),
            rows,
            P(),
            P(),
            P(),
            P(None, "tensor"),
            P("tensor"),
            rows,
            P(),
            P(),
            P(),
            P(None, ("dp", "tensor")),
            P("dp", None),
            P("dp", None),
            both,
        ),
        out_specs=(
            *(both,) * 7,
            P(),
            P(),
            rows,
            P("tensor"),
            rows,
            rows,
            P("tensor"),
            rows,
            P(),
            P(),
            P(),
            P(None, "tensor"),
            P("tensor"),
            rows,
            P(),
            P(),
            P(),
        ),
        check_vma=False,
    )
```

profile of v0, /device:TPU:0, one launch (start us, length us, event | category | flops | bytes accessed | tf_op | source)
XLA Modules:
  0.0 304.7 jit_solution(17921299783756145922)
XLA Ops:
  0.7 0.0 copy-start.3
  0.7 0.0 copy-start.4
  0.7 0.0 copy-start.5
  0.7 0.0 copy-start.6
  0.7 0.0 copy-start.7
  0.7 0.0 copy-start.8
  0.7 0.0 copy-start.9
  0.7 0.0 copy-start.10
  0.7 0.0 copy-start.11
  0.8 0.0 copy-start.12
  0.8 0.0 copy-start.13
  0.8 0.8 constant_dynamic-update-slice_fusion.4
  1.6 0.8 constant_dynamic-update-slice_fusion.3
  2.4 0.8 constant_dynamic-update-slice_fusion.2
  3.2 0.8 constant_dynamic-update-slice_fusion.1
  4.0 0.8 constant_dynamic-update-slice_fusion.slab
  4.8 0.0 copy-start.2
  4.8 2.4 pad_maximum_fusion.square
  7.2 0.0 copy-done.3
  7.2 0.0 copy-done.4
  7.2 0.0 copy-done.5
  7.2 0.0 copy-done.6
  7.3 0.0 copy-done.7
  7.3 0.0 copy-done.8
  7.3 0.0 copy-done.9
  7.3 0.0 copy-done.10
  7.3 0.0 copy-done.11
  7.4 0.0 copy-done.12
  7.4 0.0 copy-done.13
  7.4 0.1 pad_maximum_fusion.1
  7.5 1.3 stack.51.vectors
  8.8 0.0 copy-done.2
  8.8 108.7 %forward_all.1 = (f32[512,768]{1,0:T(8,128)}, f32[512,768]{1,0:T(8,128)}, f32[8,768]{1,0:T(8,128)}, bf16[3,4,768,768]{3,2,1,0:T(8,128)(2,1)}, bf16[512,768]{1,0:...) custom-call(bf16[144,768]{1,0:T(8,128)(2,1)} %copy-done.2, ...), custom_call_target="tpu_custom_call" | custom-call | tf_op jit(solution)/shard_map/forward_all/pallas_call | solution.py:641
  117.4 172.7 %backward_all.1 = (f32[512,768]{1,0:T(8,128)}, bf16[9,256,768]{2,1,0:T(8,128)(2,1)}, bf16[144,768]{1,0:T(8,128)(2,1)}, f32[16,768]{1,0:T(8,128)}) custom-call(bf16[3,4,768,768]{3,2,1,0:T(8,128)(2,1)} %get-tuple-element.44.weights_in, f32[16,768]{1,0:T(8,128)} %stack.51.vectors, s32[4,512]{1,0:T(4,128)} %boxes.3, s32[4,512]{1,0:T(4,128)} %segments.3, ...), custom_call_target="tpu_custom_call" | custom-call | tf_op jit(solution)/shard_map/backward_all/pallas_call | solution.py:1252
  290.1 1.4 slice.87
  291.5 1.6 fusion.2
  293.1 1.7 slice_reduce_fusion
  294.8 4.7 %fusion = (f32[3,256,768]{2,1,0:T(8,128)}, f32[3,256,768]{2,1,0:T(8,128)}, f32[3,256,768]{2,1,0:T(8,128)S(1)}) fusion(bf16[9,256,768]{2,1,0:T(8,128)(2,1)} %get-tuple-element.61), kind=kLoop, calls=%fused_computation.17 | loop fusion | bytes 14155776 | tf_op jit(solution)/shard_map/unstack | solution.py:1373
  299.5 0.0 copy-start
  299.5 1.4 fusion.1
  300.9 0.0 copy-start.1
  300.9 1.5 fusion.3
  302.4 0.0 copy-done
  302.4 1.1 copy.57
  303.6 0.0 copy-done.1
  303.6 1.1 copy.58
  (13 shorter events, 0.1 us)
Async XLA Ops:
  0.7 6.5 %copy-start.3 = (f32[768]{0:T(1024)S(1)}, f32[768]{0:T(1024)}, u32[]{:S(2)}) copy-start(f32[768]{0:T(1024)} %param.33) | copy-start | bytes 9220
  0.7 6.5 %copy-start.4 = (f32[768]{0:T(1024)S(1)}, f32[768]{0:T(1024)}, u32[]{:S(2)}) copy-start(f32[768]{0:T(1024)} %param.34) | copy-start | bytes 9220
  0.7 6.5 %copy-start.5 = (f32[768]{0:T(1024)S(1)}, f32[768]{0:T(1024)}, u32[]{:S(2)}) copy-start(f32[768]{0:T(1024)} %param.41) | copy-start | bytes 9220
  0.7 6.5 %copy-start.6 = (f32[768]{0:T(1024)S(1)}, f32[768]{0:T(1024)}, u32[]{:S(2)}) copy-start(f32[768]{0:T(1024)} %param.42) | copy-start | bytes 9220
  0.7 6.6 %copy-start.7 = (f32[768]{0:T(1024)S(1)}, f32[768]{0:T(1024)}, u32[]{:S(2)}) copy-start(f32[768]{0:T(1024)} %param.43) | copy-start | bytes 9220
  0.7 6.6 %copy-start.8 = (f32[768]{0:T(1024)S(1)}, f32[768]{0:T(1024)}, u32[]{:S(2)}) copy-start(f32[768]{0:T(1024)} %param.47) | copy-start | bytes 9220
  0.7 6.6 %copy-start.9 = (f32[768]{0:T(1024)S(1)}, f32[768]{0:T(1024)}, u32[]{:S(2)}) copy-start(f32[768]{0:T(1024)} %param.48) | copy-start | bytes 9220
  0.7 6.6 %copy-start.10 = (f32[768]{0:T(1024)S(1)}, f32[768]{0:T(1024)}, u32[]{:S(2)}) copy-start(f32[768]{0:T(1024)} %param.49) | copy-start | bytes 9220
  0.7 6.6 %copy-start.11 = (f32[768]{0:T(1024)S(1)}, f32[768]{0:T(1024)}, u32[]{:S(2)}) copy-start(f32[768]{0:T(1024)} %param.45) | copy-start | bytes 9220
  0.8 6.6 %copy-start.12 = (f32[192]{0:T(256)S(1)}, f32[192]{0:T(256)}, u32[]{:S(2)}) copy-start(f32[192]{0:T(256)} %param.39) | copy-start | bytes 2308
  0.8 6.6 %copy-start.13 = (f32[192]{0:T(256)S(1)}, f32[192]{0:T(256)}, u32[]{:S(2)}) copy-start(f32[192]{0:T(256)} %param.36) | copy-start | bytes 2308
  4.8 4.0 %copy-start.2 = (bf16[144,768]{1,0:T(8,128)(2,1)}, bf16[144,768]{1,0:T(8,128)(2,1)S(1)}, u32[]{:S(2)}) copy-start(bf16[144,768]{1,0:T(8,128)(2,1)S(1)} %constant_dynamic-update-slice_fusion.slab) | copy-start | bytes 663556
  299.5 2.9 copy-start
  300.9 2.6 copy-start.1
where the time goes:
time: 305 us
  Pallas kernels  281 us (92%)
  local copies, waits for them, and re-layouts  20 us (7%)
    pallas_call x1, Pallas kernels, backward_all(): pl.pallas_call(functools.partial(backward_kernel, bits, owns, slab_rows),...  173 us
    pallas_call x1, Pallas kernels, forward_all(): pl.pallas_call(functools.partial(forward_kernel, bits, owns), out_shape=[...  109 us

commit v1 on v0

--- a/solution.py
+++ b/solution.py
@@ -93,6 +93,12 @@
     def finish(self):
         for copy in self.sent:
             copy.wait_send()
+
+
+def seldom(steps, times):
+    for _ in steps:
+        for _ in range(times):
+            yield
 
 
 def interleave(*steps):
@@ -202,11 +208,12 @@
 CHUNKS = 2
 
 
-def chunk_rows(place, weights, j, near):
-    side = weights.shape[2] // 2
+def chunk_rows(place, weights, j, near_row, near_line):
+    side = weights.shape[2] // 4
     rows = side // CHUNKS
-    row_bit = place.bit(0) if near else 1 - place.bit(0)
-    start = row_bit * side + (j % CHUNKS) * rows
+    row = place.bit(0) if near_row else 1 - place.bit(0)
+    line = place.bit(1) if near_line else 1 - place.bit(1)
+    start = (2 * row + line) * side + (j % CHUNKS) * rows
     return j // CHUNKS, pl.ds(pl.multiple_of(start, rows), rows)
 
 
@@ -219,8 +226,8 @@
         self.own_send = own_send
         self.own_recv = own_recv
 
-    def copy(self, way, lane, j, t, near, to=None):
-        matrix, rows = chunk_rows(self.place, self.weights, j, near)
+    def copy(self, way, lane, j, t, near_row=True, near_line=True):
+        matrix, rows = chunk_rows(self.place, self.weights, j, near_row, near_line)
         block = self.weights.at[matrix, t, rows]
         return pltpu.make_async_remote_copy(
             src_ref=block,
@@ -254,33 +261,47 @@
         ).wait_recv()
 
     def issue(self, j):
-        self.copy("half", 0, j, self.place.t, True).start()
+        self.copy("half", 0, j, self.place.t).start()
 
     def take_half(self, j):
         other = self.place.t_flip(2)
-        self.copy("half", 0, j, other, True).wait_recv()
-        self.copy(0, 1, j, other, True).start()
-        self.copy("core", 2, j, other, True).start()
+        self.copy("half", 0, j, other).wait_recv()
+        self.copy(0, 1, j, other).start()
+        self.copy(1, 2, j, other).start()
+        self.copy("core", 4, j, other).start()
 
     def take_row(self, j):
         other = self.place.t_flip(2)
         self.copy(0, 1, j, other, False).wait_recv()
-        self.copy("core", 3, j, other, False).start()
+        self.copy(1, 3, j, other, False).start()
+        self.copy("core", 5, j, other, False).start()
+
+    def take_line(self, j):
+        other = self.place.t_flip(2)
+        for lane, near_row in ((2, True), (3, False)):
+            self.copy(1, lane, j, other, near_row, False).wait_recv()
+            self.copy("core", lane + 4, j, other, near_row, False).start()
 
     def settle(self, j):
         cross = self.place.t_flip(3)
-        self.copy("core", 2, j, cross, True).wait_recv()
-        self.copy("core", 3, j, cross, False).wait_recv()
+        for lane, near_row, near_line in self.core_lanes():
+            self.copy("core", lane, j, cross, near_row, near_line).wait_recv()
+
+    def core_lanes(self):
+        return ((4, True, True), (5, False, True), (6, True, False), (7, False, False))
 
     def finish(self, count):
         for i in range(3):
             self.own(i).wait_send()
 
         def one(j, carry):
-            self.copy("half", 0, j, self.place.t, True).wait_send()
-            self.copy(0, 1, j, self.place.t_flip(2), True).wait_send()
-            self.copy("core", 2, j, self.place.t_flip(2), True).wait_send()
-            self.copy("core", 3, j, self.place.t_flip(2), False).wait_send()
+            other = self.place.t_flip(2)
+            self.copy("half", 0, j, self.place.t).wait_send()
+            self.copy(0, 1, j, other).wait_send()
+            self.copy(1, 2, j, other).wait_send()
+            self.copy(1, 3, j, other, False).wait_send()
+            for lane, near_row, near_line in self.core_lanes():
+                self.copy("core", lane, j, other, near_row, near_line).wait_send()
             return carry
 
         lax.fori_loop(0, count, one, 0)
@@ -365,8 +386,23 @@
 def forward_kernel(
     bits,
     owns,
-    slab,
-    square,
+    slab_rows,
+    pieces,
+    *refs,
+):
+    slabs, refs = refs[:pieces], refs[pieces:]
+    forward_body(bits, owns, slab_rows, slabs, *refs)
+
+
+def forward_body(
+    bits,
+    owns,
+    slab_rows,
+    slabs,
+    w_query,
+    w_key,
+    w_value,
+    w_out,
     wide,
     tall,
     vectors,
@@ -379,15 +415,23 @@
     grad_sum,
     grad_vectors,
     weights_out,
+    inputs_low_out,
+    centered_in_out,
+    scaled_in,
+    projected_out,
+    mixed_out,
+    stats,
+    mid_low_out,
+    centered_mid_out,
+    scaled_mid,
+    hidden_out,
+    slopes_out,
     inputs_low,
     centered_in,
-    scaled_in,
     projected,
     mixed,
-    stats,
     mid_low,
     centered_mid,
-    scaled_mid,
     hidden,
     slopes,
     tables,
@@ -409,34 +453,45 @@
     own_recv,
     bias_sems,
     local_sems,
+    own_sems,
+    ship_sems,
 ):
     place = Place(bits)
     tokens, width = word.shape
     dps = 2**bits
-    slab_rows = slab.shape[0]
     t = place.t
+    me = place.dp * 4 + t
+    local = copies_into(tables.at[me], slabs, own_sems.at[3])
+    owned = [
+        copies_into(weights.at[i, t], sources, own_sems.at[i])
+        for i, sources in enumerate(((w_query, w_key, w_value, w_out), (wide,), (tall,)))
+    ]
+    for copy in local + owned[0] + owned[1] + owned[2]:
+        copy.start()
+    shipped = []
+
+    def ship(source, target):
+        copy = pltpu.make_async_copy(source, target, ship_sems.at[len(shipped)])
+        copy.start()
+        shipped.append(copy)
+
     place.greet()
     links = Links(place, send_sems)
     flow = Weights(place, weights, weight_send, weight_recv, own_send, own_recv)
     chunks = 3 * CHUNKS
-    local = pltpu.make_async_copy(slab, tables.at[place.dp * 4 + t], local_sems.at[3])
-    local.start()
-    owned = [
-        pltpu.make_async_copy(source, weights.at[i, t], local_sems.at[i])
-        for i, source in enumerate((square, wide, tall))
-    ]
-    for copy in owned:
-        copy.start()
+    for copy in local:
+        copy.wait()
     gather = tables_gather(
-        place, links, slab, tables, (line_sem, half_sem, row_sem, cross_sem, core_sem)
+        place, links, tables.at[me], tables, (line_sem, half_sem, row_sem, cross_sem, core_sem)
     )
     next(gather)
     bias = vectors.at[pl.ds(8, 8)]
     biases[t] = vectors[8:16]
     links.send("core", bias, biases.at[t], bias_sems.at[0])
     links.send("half", bias, biases.at[t], bias_sems.at[1])
-    for i, copy in enumerate(owned):
-        copy.wait()
+    for i, copies in enumerate(owned):
+        for copy in copies:
+            copy.wait()
         flow.own(i).start()
     flow.issue(0)
     flow.issue(1)
@@ -453,8 +508,6 @@
     lax.fori_loop(0, dps, count_dp, 0)
     mask_pages(seg, masks)
     total[...] = word[...].astype(F32)
-    local.wait()
-
     def embed(row_bit):
         def one(i, carry):
             dp = 2 * i + row_bit
@@ -474,11 +527,15 @@
     embed(place.bit(0))
     flow.take_half(1)
     flow.issue(3)
+    flow.take_row(0)
     for step in gather:
         pass
-    flow.take_row(0)
+    flow.take_row(1)
+    flow.take_line(0)
     embed(1 - place.bit(0))
-    flow.take_row(1)
+    flow.take_half(2)
+    flow.issue(4)
+    flow.take_line(1)
 
     def norm_in(rows):
         centered, scaled = norm_parts(total[rows])
@@ -489,6 +546,11 @@
         inputs_low[rows] = result.astype(BF16)
 
     by_rows(tokens, norm_in)
+    ship(inputs_low, inputs_low_out)
+    ship(centered_in, centered_in_out)
+    flow.take_half(3)
+    flow.issue(5)
+    flow.take_row(2)
     links.arrived("core", biases.at[place.t_flip(1)], bias_sems.at[0])
     links.arrived("core", biases.at[place.t_flip(3)], bias_sems.at[2])
     flow.own_arrived(0)
@@ -508,8 +570,9 @@
         return carry
 
     lax.fori_loop(0, 4, project, 0)
-    flow.take_half(2)
-    flow.issue(4)
+    ship(projected, projected_out)
+    flow.take_half(4)
+    flow.take_row(3)
 
     def attend(j, carry):
         for h in range(fourth // HEAD):
@@ -537,25 +600,25 @@
     def attend_and_pass(j, carry):
         attend(j, carry)
 
+        @pl.when(j < 1)
+        def _():
+            flow.take_half(5)
+
         @pl.when(j < 2)
         def _():
-            flow.take_row(j + 2)
-
-        @pl.when(j < 2)
+            flow.take_row(j + 4)
+
+        @pl.when(j < 3)
         def _():
-            flow.take_half(j + 3)
-
-        @pl.when(j < 1)
-        def _():
-            flow.issue(j + 5)
+            flow.take_line(j + 2)
 
         return carry
 
     lax.fori_loop(0, 4, attend_and_pass, 0)
+    ship(mixed, mixed_out)
     out_rows = weights[0, :, 3 * fourth :, :].reshape(width, width)
     total[...] = inner_rows(mixed[...].reshape(width, tokens), out_rows)
-    flow.take_row(4)
-    flow.take_half(5)
+    flow.take_line(5)
 
     def norm_mid(rows):
         centered, scaled = norm_parts(total[rows] + vectors[2:3] + normed[rows])
@@ -566,8 +629,16 @@
         mid_low[rows] = result.astype(BF16)
 
     by_rows(tokens, norm_mid)
+    ship(mid_low, mid_low_out)
+    ship(centered_mid, centered_mid_out)
     total[...] = jnp.zeros_like(total)
     columns = 256
+
+    def feed_copies(j):
+        return [
+            pltpu.make_async_copy(source.at[j], target.at[j], local_sems.at[1 + i, j])
+            for i, (source, target) in enumerate(((hidden, hidden_out), (slopes, slopes_out)))
+        ]
 
     def feed(j):
         def one(n, carry):
@@ -581,6 +652,8 @@
 
         lax.fori_loop(0, width // columns, one, 0)
         total[...] += product(hidden[j], weights[2, j])
+        for copy in feed_copies(j):
+            copy.start()
 
     flow.own_arrived(1)
     flow.own_arrived(2)
@@ -590,10 +663,9 @@
         return carry
 
     lax.fori_loop(0, 2, feed_near, 0)
-    flow.take_row(5)
     for j in range(CHUNKS, chunks):
         flow.settle(j)
-    out_copy = pltpu.make_async_copy(weights, weights_out, local_sems.at[0])
+    out_copy = pltpu.make_async_copy(weights, weights_out, local_sems.at[0, 0])
     out_copy.start()
 
     def feed_far(i, carry):
@@ -614,6 +686,11 @@
 
     by_rows(tokens, norm_out)
     out_copy.wait()
+    for copy in shipped:
+        copy.wait()
+    for j in range(4):
+        for copy in feed_copies(j):
+            copy.wait()
     links.finish()
     flow.finish(chunks)
 
@@ -626,8 +703,19 @@
     return scaled * (grad_centered - first_mean - centered * second_mean)
 
 
+def copies_into(target, sources, sems):
+    first, copies = 0, []
+    for i, source in enumerate(sources):
+        rows = source.shape[0]
+        copies.append(
+            pltpu.make_async_copy(source, target.at[pl.ds(first, rows)], sems.at[i])
+        )
+        first += rows
+    return copies
+
+
 def forward_all(
-    devices, owns, slab, square, wide, tall, vectors, word, boxes, segments, offsets, cotangent
+    devices, owns, slab_rows, slabs, matrices, vectors, word, boxes, segments, offsets, cotangent
 ):
     bits = (devices // 4).bit_length() - 1
     dps = 2**bits
@@ -635,11 +723,10 @@
     tokens, width = word.shape
     anywhere = pl.BlockSpec(memory_space=pl.ANY)
     in_vmem = pl.BlockSpec(memory_space=pltpu.VMEM)
-    slab_rows = slab.shape[0]
     fourth = width // 4
     shape = jax.ShapeDtypeStruct
     return pl.pallas_call(
-        functools.partial(forward_kernel, bits, owns),
+        functools.partial(forward_kernel, bits, owns, slab_rows, len(slabs)),
         out_shape=[
             shape((tokens, width), F32),
             shape((tokens, width), F32),
@@ -657,9 +744,24 @@
             shape((4, tokens, width), BF16),
             shape((4, tokens, width), BF16),
         ],
-        in_specs=[anywhere] * 4 + [in_vmem] * 6,
-        out_specs=[in_vmem] * 3 + [anywhere] + [in_vmem] * 11,
+        in_specs=[anywhere] * (len(slabs) + len(matrices)) + [in_vmem] * 6,
+        out_specs=[in_vmem] * 3
+        + [anywhere] * 3
+        + [in_vmem]
+        + [anywhere] * 2
+        + [in_vmem]
+        + [anywhere] * 2
+        + [in_vmem]
+        + [anywhere] * 2,
         scratch_shapes=[
+            pltpu.VMEM((tokens, width), BF16),
+            pltpu.VMEM((tokens, width), BF16),
+            pltpu.VMEM((4, 3 * fourth, tokens), BF16),
+            pltpu.VMEM((4, fourth, tokens), BF16),
+            pltpu.VMEM((tokens, width), BF16),
+            pltpu.VMEM((tokens, width), BF16),
+            pltpu.VMEM((4, tokens, width), BF16),
+            pltpu.VMEM((4, tokens, width), BF16),
             pltpu.VMEM((devices, slab_rows, width), BF16),
             pltpu.VMEM((dps, 4 * slab_rows, tokens), BF16),
             pltpu.VMEM((3, 4, width, width), BF16),
@@ -673,18 +775,20 @@
             pltpu.SemaphoreType.DMA((lines,)),
             pltpu.SemaphoreType.DMA((lines,)),
             pltpu.SemaphoreType.DMA((4 * lines,)),
-            pltpu.SemaphoreType.DMA((4, 3 * CHUNKS)),
-            pltpu.SemaphoreType.DMA((4, 3 * CHUNKS)),
+            pltpu.SemaphoreType.DMA((8, 3 * CHUNKS)),
+            pltpu.SemaphoreType.DMA((8, 3 * CHUNKS)),
             pltpu.SemaphoreType.DMA((3,)),
             pltpu.SemaphoreType.DMA((3,)),
             pltpu.SemaphoreType.DMA((3,)),
-            pltpu.SemaphoreType.DMA((4,)),
+            pltpu.SemaphoreType.DMA((3, 4)),
+            pltpu.SemaphoreType.DMA((4, max(4, len(slabs)))),
+            pltpu.SemaphoreType.DMA((6,)),
         ],
         name="forward_all",
         compiler_params=pltpu.CompilerParams(
             collective_id=0, has_side_effects=True, vmem_limit_bytes=60 * 2**20
         ),
-    )(slab, square, wide, tall, vectors, word, boxes, segments, offsets, cotangent)
+    )(*slabs, *matrices, vectors, word, boxes, segments, offsets, cotangent)
 
 
 def ladder(rows, bits):
@@ -696,6 +800,7 @@
 
 
 SLOTS = 3
+DEPTH = 3
 PARTS = 3
 
 
@@ -713,6 +818,9 @@
         self.rows = own.shape[2]
         self.left = ladder(self.rows, place.bits)
         self.back = [b for b in range(place.bits) if self.left[b + 1] < self.left[b]]
+        self.taken = 0
+        self.issued = 0
+        self.ticks = 0
 
     def copy(self, way, lane, j, src, dst):
         return pltpu.make_async_remote_copy(
@@ -772,9 +880,24 @@
             pl.semaphore_signal(
                 self.credit, inc=1, device_id=self.place.partner("core"), device_id_type=MESH
             )
+        self.taken = j + 1
+        self.pump()
+
+    def pump(self):
+        while self.issued < min(self.taken, self.ticks + DEPTH):
+            self.half(self.issued).start()
+            self.issued += 1
+
+    def tick(self, count):
+        k = self.ticks
+        self.ticks += 1
+        for s in range(self.stages()):
+            if 0 <= k - s < count:
+                self.stage(s, k - s)
 
     def take_half(self, j):
         self.half(j).wait_recv()
+        self.pump()
         span = self.span(0, False)
         self.own[j, 0, span] = added(self.own[j, 0, span], self.from_half[j, span])
         self.dp(0, j).start()
@@ -829,78 +952,46 @@
         lax.fori_loop(0, count, one, 0)
 
 
-def table_reduce(place, links, slab_at, width_of, columns, order, halves, lines, half_sems, dp_sems):
+def table_reduce(place, links, slab_at, columns, order, landing, sems):
     bits = place.bits
-
-    def slab(mask, half):
-        return slab_at(place.dp_flip(mask), half).at[:, columns]
-
-    def add(mask, half, landed):
-        target = slab(mask, half)
-        target[...] = added(target[...], landed[...])
-
-    def lowest(mask):
-        return (mask & -mask).bit_length() - 1 if mask else bits
-
-    mine, theirs = place.half, 1 - place.half
-    masks = sorted(range(2**bits), key=lambda m: (lowest(m), m))
-    slot = 0
-    base = {}
-    for b in range(bits):
-        for h in range(2 if (b == 0 and order == "row") else 1):
-            base[b, h] = slot
-            slot += 2 ** (bits - 1 - b)
-
-    def index(b, h, mask):
-        return base[b, h] + (mask >> (b + 1))
-
-    def send_dp(b, mask, half, h):
-        i = index(b, h, mask ^ (1 << b))
-        links.send(b, slab(mask, half), lines.at[i], dp_sems.at[i])
-
-    def take_dp(b, mask, half, h):
-        i = index(b, h, mask)
-        links.arrived(b, lines.at[i], dp_sems.at[i])
-        add(mask, half, lines.at[i])
-
-    if order == "half":
-        for mask in masks:
-            links.send("half", slab(mask, theirs), halves.at[mask], half_sems.at[mask])
-        yield
-        for mask in masks:
-            links.arrived("half", halves.at[mask], half_sems.at[mask])
-            add(mask, mine, halves.at[mask])
-            if mask & 1:
-                send_dp(0, mask, mine, 0)
-            yield
-    else:
-        for h, half in ((1, theirs), (0, mine)):
-            for mask in masks:
-                if mask & 1:
-                    send_dp(0, mask, half, h)
-        yield
-        kept = [m for m in masks if not m & 1]
-        for mask in kept:
-            take_dp(0, mask, theirs, 1)
-            links.send("half", slab(mask, theirs), halves.at[mask], half_sems.at[mask])
-            yield
-        for mask in kept:
-            take_dp(0, mask, mine, 0)
-            yield
-        for mask in kept:
-            links.arrived("half", halves.at[mask], half_sems.at[mask])
-            add(mask, mine, halves.at[mask])
-            if bits > 1 and mask & 2:
-                send_dp(1, mask, mine, 0)
-            yield
-    for b in range(0 if order == "half" else 1, bits):
-        for mask in masks:
-            if mask % (2 << b):
-                continue
-            take_dp(b, mask, mine, 0)
-            if b + 1 < bits and mask & (2 << b):
-                send_dp(b + 1, mask, mine, 0)
-            yield
+    flags = [1 << (bits if way == "half" else way) for way in order]
+
+    def slab(mask):
+        half = 1 - place.half if mask >> bits else place.half
+        return slab_at(place.dp_flip(mask % (1 << bits)), half).at[:, columns]
+
+    def first(mask):
+        for i, flag in enumerate(flags):
+            if mask & flag:
+                return i
+        return len(flags)
+
+    every = sorted(range(2 ** (bits + 1)), key=lambda m: (first(m), m))
+    slots = {}
+    for i in range(len(flags)):
+        for mask in every:
+            if first(mask) > i:
+                slots[i, mask] = len(slots)
+
+    def send(i, mask):
+        slot = slots[i, mask ^ flags[i]]
+        links.send(order[i], slab(mask), landing.at[slot], sems.at[slot])
+
+    for mask in sorted(
+        (m for m in every if first(m) == 0), key=lambda m: (first(m ^ flags[0]), m)
+    ):
+        send(0, mask)
+    yield
+    for i in range(len(flags)):
+        for mask in every:
+            if first(mask) > i:
+                slot = slots[i, mask]
+                links.arrived(order[i], landing.at[slot], sems.at[slot])
+                target = slab(mask)
+                target[...] = added(target[...], landing[slot])
+                if first(mask) == i + 1 < len(flags):
+                    send(i + 1, mask)
+                yield
 
 
 def vector_reduce(place, links, vectors, landing, sems):
@@ -922,14 +1013,14 @@
     offsets,
     grad_sum,
     ffn_vectors,
-    inputs_low,
-    centered_in,
+    inputs_low_in,
+    centered_in_in,
     scaled_in,
-    projected,
-    mixed,
+    projected_in,
+    mixed_in,
     stats,
-    mid_low,
-    centered_mid,
+    mid_low_in,
+    centered_mid_in,
     scaled_mid,
     hidden_in,
     slopes_in,
@@ -938,6 +1029,12 @@
     table_sum,
     vector_sum,
     held,
+    inputs_low,
+    centered_in,
+    projected,
+    mixed,
+    mid_low,
+    centered_mid,
     hidden,
     slopes,
     outgoing,
@@ -945,9 +1042,7 @@
     from_core,
     from_half,
     from_dp,
-    halves,
-    lines_half,
-    lines_row,
+    landing,
     words,
     lookups,
     vector_terms,
@@ -961,12 +1056,11 @@
     send_sems,
     sum_send,
     sum_recv,
-    half_sems,
-    line_half_sems,
-    line_row_sems,
+    landing_sems,
     vector_sems,
     word_sems,
     local_sems,
+    later_sems,
     credit,
 ):
     place = Place(bits)
@@ -990,7 +1084,20 @@
         pltpu.make_async_copy(hidden_in, hidden, local_sems.at[3, 0]),
         pltpu.make_async_copy(slopes_in, slopes, local_sems.at[3, 1]),
     ]
-    for copy in loads[2] + early + loads[1]:
+    later = [
+        pltpu.make_async_copy(source, target, later_sems.at[i])
+        for i, (source, target) in enumerate(
+            (
+                (mid_low_in, mid_low),
+                (centered_mid_in, centered_mid),
+                (projected_in, projected),
+                (mixed_in, mixed),
+                (inputs_low_in, inputs_low),
+                (centered_in_in, centered_in),
+            )
+        )
+    ]
+    for copy in loads[2] + early + loads[1] + later:
         copy.start()
     place.greet()
     links = Links(place, send_sems)
@@ -1053,17 +1160,18 @@
         chunk(p, functools.partial(down_term, p))
         if p:
             sums.take_core(p - 1, chunks)
-            sums.half(p - 1).start()
     for copy in loads[0]:
         copy.start()
     sums.take_core(PARTS - 1, chunks)
-    for copy in loads[1]:
+    for copy in loads[1] + later:
         copy.wait()
     for p in range(PARTS):
         columns = slice(p * part, (p + 1) * part)
         chunk(PARTS + p, lambda q: inner_rows(mid_low[:, columns], slopes[q]))
         if p:
             sums.take_core(PARTS + p - 1, chunks)
+        if p == PARTS - 1:
+            sums.tick(chunks)
     total[...] = grad_sum[...]
 
     def mid_term(q, carry):
@@ -1072,20 +1180,6 @@
 
     lax.fori_loop(0, 4, mid_term, 0)
     sums.take_core(2 * PARTS - 1, chunks)
-
-    done = [0]
-    stages = sums.stages()
-
-    def tick(limit):
-        k = done[0]
-        done[0] += 1
-        for s in range(stages):
-            j = k - s
-            if j < 0 or j >= limit:
-                continue
-            sums.stage(s, j)
-            if s == 0 and j + 2 < limit:
-                sums.half(j + 2).start()
 
     def mid_back(rows):
         centered = centered_mid[rows].astype(F32)
@@ -1106,6 +1200,7 @@
         return carry
 
     lax.fori_loop(0, 4, out_back, 0)
+    sums.tick(chunks)
     scale = HEAD ** (-0.5)
 
     def attend_back(j, carry):
@@ -1149,7 +1244,7 @@
 
     for j in (0, 2):
         lax.fori_loop(j, j + 2, attend_back, 0)
-        tick(chunks)
+        sums.tick(chunks)
 
     def square_term(p, q):
         if p < PARTS - 1:
@@ -1187,48 +1282,55 @@
     word_copy.start()
     links.send("core", low, words, word_sems.at[1])
     links.arrived("core", lookups.at[1], word_sems.at[0])
-    tick(chunks)
+    sums.tick(chunks)
     links.arrived("core", words, word_sems.at[1])
 
     def slab_at(dp, half):
         start = (dp * 2 + half) * slab_rows
         return held.at[pl.ds(pl.multiple_of(start, 16), slab_rows)]
 
-    def table_term(dp, carry):
-        for i in range(2):
-            rows = tuple(lookups[i, w : w + 1, :] for w in range(7))
-            for h in range(2):
-                counts[i, h * slab_rows : (h + 1) * slab_rows, :] = row_counts(
-                    rows, dp * 4 + h * 2 + core, owns, slab_rows, tokens
-                )
-        start = pl.multiple_of(dp * 2 * slab_rows, 16)
-        held[pl.ds(start, 2 * slab_rows)] = (
-            product(counts[0], low[...]) + product(counts[1], words[...])
-        ).astype(BF16)
-        return carry
-
-    lax.fori_loop(0, dps, table_term, 0)
+    def table_term(row_bit):
+        def one(n, carry):
+            dp = 2 * n + row_bit
+            for i in range(2):
+                rows = tuple(lookups[i, w : w + 1, :] for w in range(7))
+                for h in range(2):
+                    counts[i, h * slab_rows : (h + 1) * slab_rows, :] = row_counts(
+                        rows, dp * 4 + h * 2 + core, owns, slab_rows, tokens
+                    )
+            start = pl.multiple_of(dp * 2 * slab_rows, 16)
+            held[pl.ds(start, 2 * slab_rows)] = (
+                product(counts[0], low[...]) + product(counts[1], words[...])
+            ).astype(BF16)
+            return carry
+
+        lax.fori_loop(0, dps // 2, one, 0)
+
     split = width // 2
-    steps = [
+    lines = list(range(1, bits))
+    by_row, by_line = (
         table_reduce(
-            place, links, slab_at, width, pl.ds(0, split), "half",
-            halves.at[0], lines_half, half_sems.at[0], line_half_sems,
-        ),
-        table_reduce(
-            place, links, slab_at, width, pl.ds(split, split), "row",
-            halves.at[1], lines_row, half_sems.at[1], line_row_sems,
-        ),
-        vector_reduce(place, links, vector_terms, vector_land, vector_sems),
-    ]
+            place, links, slab_at, pl.ds(i * split, split), order, landing.at[i], landing_sems.at[i]
+        )
+        for i, order in enumerate(([0, "half"] + lines, lines + ["half", 0]))
+    )
+    table_term(1 - place.bit(0))
+    next(by_row)
+    table_term(place.bit(0))
+    next(by_line)
 
     def ticks():
-        while done[0] < chunks + stages - 1:
-            tick(chunks)
-            yield
-            yield
-            yield
-
-    interleave(ticks(), *steps)
+        while sums.ticks < chunks + sums.stages() - 1:
+            sums.tick(chunks)
+            for _ in range(3):
+                yield
+
+    interleave(
+        ticks(),
+        by_row,
+        by_line,
+        seldom(vector_reduce(place, links, vector_terms, vector_land, vector_sems), 3),
+    )
     table_sum[...] = slab_at(place.dp, place.half)[...]
     vector_sum[...] = vector_terms[bits + 2]
     word_copy.wait()
@@ -1245,8 +1347,6 @@
     fourth, part = width // 4, width // PARTS
     chunks = 3 * PARTS
     landing = sum(ladder(part, bits)[1:])
-    half_lines = dps - 1
-    row_lines = dps - 1 + dps // 2
     held_rows = max(8 * width, 2 * dps * slab_rows)
     shape = jax.ShapeDtypeStruct
     return pl.pallas_call(
@@ -1257,10 +1357,24 @@
             shape((slab_rows, width), BF16),
             shape((16, width), F32),
         ],
-        in_specs=[anywhere] + [in_vmem] * (2 + len(kept)) + [anywhere] * 2,
+        in_specs=[anywhere]
+        + [in_vmem] * 6
+        + [anywhere] * 2
+        + [in_vmem]
+        + [anywhere] * 2
+        + [in_vmem]
+        + [anywhere] * 2
+        + [in_vmem]
+        + [anywhere] * 2,
         out_specs=[anywhere] + [in_vmem] * 3,
         scratch_shapes=[
             pltpu.VMEM((held_rows, width), BF16),
+            pltpu.VMEM((tokens, width), BF16),
+            pltpu.VMEM((tokens, width), BF16),
+            pltpu.VMEM((4, 3 * fourth, tokens), BF16),
+            pltpu.VMEM((4, fourth, tokens), BF16),
+            pltpu.VMEM((tokens, width), BF16),
+            pltpu.VMEM((tokens, width), BF16),
             pltpu.VMEM((4, tokens, width), BF16),
             pltpu.VMEM((4, tokens, width), BF16),
             pltpu.VMEM((SLOTS, 2, part, width), BF16),
@@ -1268,9 +1382,7 @@
             pltpu.VMEM((SLOTS, 2, part, width), BF16),
             pltpu.VMEM((chunks, part, width), BF16),
             pltpu.VMEM((chunks, landing, width), BF16),
-            pltpu.VMEM((2, dps, slab_rows, width // 2), BF16),
-            pltpu.VMEM((half_lines, slab_rows, width // 2), BF16),
-            pltpu.VMEM((row_lines, slab_rows, width // 2), BF16),
+            pltpu.VMEM((2, 2 * dps - 1, slab_rows, width // 2), BF16),
             pltpu.VMEM((tokens, width), BF16),
             pltpu.VMEM((2, 8, tokens), jnp.int32),
             pltpu.VMEM((bits + 3, 16, width), F32),
@@ -1284,12 +1396,11 @@
             pltpu.SemaphoreType.DMA((6 * dps + 40,)),
             pltpu.SemaphoreType.DMA((2 + 2 * bits, chunks)),
             pltpu.SemaphoreType.DMA((2 + 2 * bits, chunks)),
-            pltpu.SemaphoreType.DMA((2, dps)),
-            pltpu.SemaphoreType.DMA((half_lines,)),
-            pltpu.SemaphoreType.DMA((row_lines,)),
+            pltpu.SemaphoreType.DMA((2, 2 * dps - 1)),
             pltpu.SemaphoreType.DMA((bits + 2,)),
             pltpu.SemaphoreType.DMA((2,)),
             pltpu.SemaphoreType.DMA((4, 4)),
+            pltpu.SemaphoreType.DMA((6,)),
             pltpu.SemaphoreType.REGULAR,
         ],
         name="backward_all",
@@ -1334,9 +1445,10 @@
     owned = (position_table, horizontal_table, vertical_table, height_table, width_table)
     slab_rows = sum(table.shape[0] for table in owned)
     slab_padded = -(-slab_rows // 16) * 16
-    slab = jnp.concatenate(owned, axis=0)
-    slab = jnp.pad(slab, ((0, slab_padded - slab_rows), (0, 0)))
-    square = jnp.concatenate((w_query, w_key, w_value, w_out), axis=0)
+    slabs = owned
+    if slab_padded > slab_rows or any(table.shape[0] % 16 for table in owned):
+        slab = jnp.concatenate(owned, axis=0)
+        slabs = (jnp.pad(slab, ((0, slab_padded - slab_rows), (0, 0))),)
     fourth = w_query.shape[0]
     bias_rows = jnp.concatenate([b_query, b_value, jnp.zeros((2 * fourth,), F32)])
     vectors = jnp.stack(
@@ -1348,10 +1460,9 @@
     layer_out, grad_ffn_sum, ffn_vectors, weights, *kept = forward_all(
         devices,
         owns,
-        slab,
-        square,
-        w_in,
-        w_down,
+        slab_padded,
+        slabs,
+        (w_query, w_key, w_value, w_out, w_in, w_down),
         vectors,
         word_vectors,
         boxes,

time: 305 us -> 279 us (0.915)
  Pallas kernels: 281 us -> 254 us
    pallas_call x1, Pallas kernels: 173 us -> 155 us  [backward_all(): pl.pallas_call(functools.partial(backward_kernel, bits, owns, slab_rows),...]
    pallas_call x1, Pallas kernels: 109 us -> 99.4 us  [forward_all(): pl.pallas_call(functools.partial(forward_kernel, bits, owns, slab_rows, l...]
    another operation x13, local copies, waits for them, and re-layouts: 1.33 us -> 7.5 us  [body(): jnp.stack([embed_gain, embed_shift, b_out, attn_gain, attn_shift, b_down,...]
    unnamed x34 -> x6, local copies, waits for them, and re-layouts: 5.55 us -> 2.29 us
where the time goes in v1:
time: 279 us; the launch traced here: 278 us
  Pallas kernels  254 us (91%)
  local copies, waits for them, and re-layouts  22.1 us (8%)
    pallas_call x1, Pallas kernels, backward_all(): pl.pallas_call(functools.partial(backward_kernel, bits, owns, slab_rows),...  155 us
    pallas_call x1, Pallas kernels, forward_all(): pl.pallas_call(functools.partial(forward_kernel, bits, owns, slab_rows, l...  99.4 us
    another operation x13, local copies, waits for them, and re-layouts, body(): jnp.stack([embed_gain, embed_shift, b_out, attn_gain, attn_shift, b_down,...  7.5 us

profile of v1, /device:TPU:0, one launch (start us, length us, event | category | flops | bytes accessed | tf_op | source)
XLA Modules:
  0.0 277.9 jit_solution(433834219823453714)
XLA Ops:
  0.7 0.7 stack.39
  1.3 0.7 stack.40
  2.0 0.7 stack.41
  2.7 0.7 stack.42
  3.4 0.7 stack.43
  4.1 0.7 stack.44
  4.8 0.7 stack.45
  5.5 0.7 stack.46
  6.2 0.7 stack.47
  6.9 0.8 pad_maximum_fusion
  7.7 1.3 stack.51.refs_11_.vectors
  8.9 99.4 %forward_all.1 = (f32[512,768]{1,0:T(8,128)}, f32[512,768]{1,0:T(8,128)}, f32[8,768]{1,0:T(8,128)}, bf16[3,4,768,768]{3,2,1,0:T(8,128)(2,1)}, bf16[512,768]{1,0:...) custom-call(bf16[16,768]{1,0:T(8,128)(2,1)} %refs_0_.1, ...), custom_call_target="tpu_custom_call" | custom-call | tf_op jit(solution)/shard_map/forward_all/pallas_call | solution.py:728
  108.3 155.0 %backward_all.1 = (f32[512,768]{1,0:T(8,128)}, bf16[9,256,768]{2,1,0:T(8,128)(2,1)}, bf16[144,768]{1,0:T(8,128)(2,1)}, f32[16,768]{1,0:T(8,128)}) custom-call(bf16[3,4,768,768]{3,2,1,0:T(8,128)(2,1)} %get-tuple-element.44.weights_in, f32[16,768]{1,0:T(8,128)} %stack.51.refs_11_.vectors, s32[4,512]{1,0:T(4,128)} %boxes.1, s32[4,512]{1,0:T(4,128)} %segments.1, ...), custom_call_target="tpu_custom_call" | custom-call | tf_op jit(solution)/shard_map/backward_all/pallas_call | solution.py:1352
  263.4 1.4 slice.87
  264.7 1.6 fusion.2
  266.3 1.7 slice_reduce_fusion
  268.1 4.7 %fusion = (f32[3,256,768]{2,1,0:T(8,128)}, f32[3,256,768]{2,1,0:T(8,128)}, f32[3,256,768]{2,1,0:T(8,128)S(1)}) fusion(bf16[9,256,768]{2,1,0:T(8,128)(2,1)} %get-tuple-element.61), kind=kLoop, calls=%fused_computation.11 | loop fusion | bytes 14155776 | tf_op jit(solution)/shard_map/unstack | solution.py:1484
  272.7 0.0 copy-start
  272.7 1.4 fusion.1
  274.2 0.0 copy-start.1
  274.2 1.5 fusion.3
  275.6 0.0 copy-done
  275.6 1.1 copy.53
  276.8 0.0 copy-done.1
  276.8 1.1 copy.54
  (4 shorter events, 0.0 us)
Async XLA Ops:
  272.7 2.9 %copy-start = (f32[512,768]{1,0:T(8,128)S(1)}, f32[512,768]{1,0:T(8,128)}, u32[]{:S(2)}) copy-start(f32[512,768]{1,0:T(8,128)} %get-tuple-element.108) | copy-start | bytes 4718596
  274.2 2.6 copy-start.1

commit v2 on v1

--- a/solution.py
+++ b/solution.py
@@ -800,7 +800,7 @@
 
 
 SLOTS = 3
-DEPTH = 3
+DEPTH = 2
 PARTS = 3
 
 
@@ -1306,29 +1306,31 @@
 
         lax.fori_loop(0, dps // 2, one, 0)
 
-    split = width // 2
+    split = width // 3
     lines = list(range(1, bits))
-    by_row, by_line = (
+    by_row, by_line, by_half = (
         table_reduce(
             place, links, slab_at, pl.ds(i * split, split), order, landing.at[i], landing_sems.at[i]
         )
-        for i, order in enumerate(([0, "half"] + lines, lines + ["half", 0]))
+        for i, order in enumerate(([0, "half"] + lines, lines + ["half", 0], ["half", 0] + lines))
     )
     table_term(1 - place.bit(0))
     next(by_row)
     table_term(place.bit(0))
     next(by_line)
+    next(by_half)
 
     def ticks():
         while sums.ticks < chunks + sums.stages() - 1:
             sums.tick(chunks)
-            for _ in range(3):
+            for _ in range(2):
                 yield
 
     interleave(
         ticks(),
         by_row,
         by_line,
+        by_half,
         seldom(vector_reduce(place, links, vector_terms, vector_land, vector_sems), 3),
     )
     table_sum[...] = slab_at(place.dp, place.half)[...]
@@ -1382,7 +1384,7 @@
             pltpu.VMEM((SLOTS, 2, part, width), BF16),
             pltpu.VMEM((chunks, part, width), BF16),
             pltpu.VMEM((chunks, landing, width), BF16),
-            pltpu.VMEM((2, 2 * dps - 1, slab_rows, width // 2), BF16),
+            pltpu.VMEM((3, 2 * dps - 1, slab_rows, width // 3), BF16),
             pltpu.VMEM((tokens, width), BF16),
             pltpu.VMEM((2, 8, tokens), jnp.int32),
             pltpu.VMEM((bits + 3, 16, width), F32),
@@ -1396,7 +1398,7 @@
             pltpu.SemaphoreType.DMA((6 * dps + 40,)),
             pltpu.SemaphoreType.DMA((2 + 2 * bits, chunks)),
             pltpu.SemaphoreType.DMA((2 + 2 * bits, chunks)),
-            pltpu.SemaphoreType.DMA((2, 2 * dps - 1)),
+            pltpu.SemaphoreType.DMA((3, 2 * dps - 1)),
             pltpu.SemaphoreType.DMA((bits + 2,)),
             pltpu.SemaphoreType.DMA((2,)),
             pltpu.SemaphoreType.DMA((4, 4)),
@@ -1451,11 +1453,10 @@
         slabs = (jnp.pad(slab, ((0, slab_padded - slab_rows), (0, 0))),)
     fourth = w_query.shape[0]
     bias_rows = jnp.concatenate([b_query, b_value, jnp.zeros((2 * fourth,), F32)])
-    vectors = jnp.stack(
+    vectors = jnp.concatenate(
         [embed_gain, embed_shift, b_out, attn_gain, attn_shift, b_down, ffn_gain, ffn_shift]
-        + [b_in, bias_rows]
-        + [jnp.zeros_like(b_in)] * 6
-    )
+        + [b_in, bias_rows, jnp.zeros((6 * width,), F32)]
+    ).reshape(16, width)
     owns = tuple(table.shape[0] for table in owned)
     layer_out, grad_ffn_sum, ffn_vectors, weights, *kept = forward_all(
         devices,

time: 279 us -> 265 us (0.950)
  Pallas kernels: 254 us -> 248 us
  local copies, waits for them, and re-layouts: 22.1 us -> 16.1 us
    another operation x13 -> x0, local copies, waits for them, and re-layouts: 7.5 us -> none  [body(): jnp.stack([embed_gain, embed_shift, b_out, attn_gain, attn_shift, b_down,...]
    pallas_call x1, Pallas kernels: 155 us -> 148 us  [backward_all(): pl.pallas_call(functools.partial(backward_kernel, bits, owns, slab_rows),...]
where the time goes in v2:
time: 265 us; the launch traced here: 264 us
  Pallas kernels  248 us (94%)
  local copies, waits for them, and re-layouts  16.1 us (6%)
    pallas_call x1, Pallas kernels, backward_all(): pl.pallas_call(functools.partial(backward_kernel, bits, owns, slab_rows),...  148 us
    pallas_call x1, Pallas kernels, forward_all(): pl.pallas_call(functools.partial(forward_kernel, bits, owns, slab_rows, l...  99.4 us

profile of v2, /device:TPU:0, one launch (start us, length us, event | category | flops | bytes accessed | tf_op | source)
XLA Modules:
  0.0 264.4 jit_solution(10246465494577051850)
XLA Ops:
  0.7 0.9 concatenate.3
  1.6 0.6 reshape.60.refs_11_.vectors
  2.2 99.4 %forward_all.1 = (f32[512,768]{1,0:T(8,128)}, f32[512,768]{1,0:T(8,128)}, f32[8,768]{1,0:T(8,128)}, bf16[3,4,768,768]{3,2,1,0:T(8,128)(2,1)}, bf16[512,768]{1,0:...) custom-call(bf16[16,768]{1,0:T(8,128)(2,1)} %refs_0_.1, ...), custom_call_target="tpu_custom_call" | custom-call | tf_op jit(solution)/shard_map/forward_all/pallas_call | solution.py:728
  101.6 148.2 %backward_all.1 = (f32[512,768]{1,0:T(8,128)}, bf16[9,256,768]{2,1,0:T(8,128)(2,1)}, bf16[144,768]{1,0:T(8,128)(2,1)}, f32[16,768]{1,0:T(8,128)}) custom-call(bf16[3,4,768,768]{3,2,1,0:T(8,128)(2,1)} %get-tuple-element.44.weights_in, f32[16,768]{1,0:T(8,128)} %reshape.60.refs_11_.vectors, s32[4,512]{1,0:T(4,128)} %boxes.1, s32[4,512]{1,0:T(4,128)} %segments.1, ...), custom_call_target="tpu_custom_call" | custom-call | tf_op jit(solution)/shard_map/backward_all/pallas_call | solution.py:1354
  249.8 1.4 slice.87
  251.2 1.6 fusion.2
  252.8 1.7 slice_reduce_fusion
  254.5 4.7 %fusion = (f32[3,256,768]{2,1,0:T(8,128)}, f32[3,256,768]{2,1,0:T(8,128)}, f32[3,256,768]{2,1,0:T(8,128)S(1)}) fusion(bf16[9,256,768]{2,1,0:T(8,128)(2,1)} %get-tuple-element.61), kind=kLoop, calls=%fused_computation.10 | loop fusion | bytes 14155776 | tf_op jit(solution)/shard_map/unstack | solution.py:1485
  259.2 0.0 copy-start
  259.2 1.4 fusion.1
  260.6 0.0 copy-start.1
  260.7 1.5 fusion.3
  262.1 0.0 copy-done
  262.1 1.1 copy.53
  263.3 0.0 copy-done.1
  263.3 1.1 copy.54
  (2 shorter events, 0.0 us)
Async XLA Ops:
  259.2 2.9 %copy-start = (f32[512,768]{1,0:T(8,128)S(1)}, f32[512,768]{1,0:T(8,128)}, u32[]{:S(2)}) copy-start(f32[512,768]{1,0:T(8,128)} %get-tuple-element.108) | copy-start | bytes 4718596
  260.6 2.6 copy-start.1

commit v3 on v2

--- a/solution.py
+++ b/solution.py
@@ -608,9 +608,9 @@
         def _():
             flow.take_row(j + 4)
 
-        @pl.when(j < 3)
+        @pl.when(j >= 1)
         def _():
-            flow.take_line(j + 2)
+            flow.take_line(j + 1)
 
         return carry
 
@@ -618,7 +618,6 @@
     ship(mixed, mixed_out)
     out_rows = weights[0, :, 3 * fourth :, :].reshape(width, width)
     total[...] = inner_rows(mixed[...].reshape(width, tokens), out_rows)
-    flow.take_line(5)
 
     def norm_mid(rows):
         centered, scaled = norm_parts(total[rows] + vectors[2:3] + normed[rows])
@@ -663,6 +662,7 @@
         return carry
 
     lax.fori_loop(0, 2, feed_near, 0)
+    flow.take_line(5)
     for j in range(CHUNKS, chunks):
         flow.settle(j)
     out_copy = pltpu.make_async_copy(weights, weights_out, local_sems.at[0, 0])

time: 265 us -> 264 us (level)
  no operation moved by 1% of the time
where the time goes in v3:
time: 264 us; the launch traced here: 262 us
  Pallas kernels  246 us (93%)
  local copies, waits for them, and re-layouts  16.1 us (6%)
    pallas_call x1, Pallas kernels, backward_all(): pl.pallas_call(functools.partial(backward_kernel, bits, owns, slab_rows),...  149 us
    pallas_call x1, Pallas kernels, forward_all(): pl.pallas_call(functools.partial(forward_kernel, bits, owns, slab_rows, l...  96.9 us

profile of v3, /device:TPU:0, one launch (start us, length us, event | category | flops | bytes accessed | tf_op | source)
XLA Modules:
  0.0 262.4 jit_solution(2628656663060666861)
XLA Ops:
  0.7 0.9 concatenate.3
  1.6 0.6 reshape.60.refs_11_.vectors
  2.2 96.9 %forward_all.1 = (f32[512,768]{1,0:T(8,128)}, f32[512,768]{1,0:T(8,128)}, f32[8,768]{1,0:T(8,128)}, bf16[3,4,768,768]{3,2,1,0:T(8,128)(2,1)}, bf16[512,768]{1,0:...) custom-call(bf16[16,768]{1,0:T(8,128)(2,1)} %refs_0_.1, ...), custom_call_target="tpu_custom_call" | custom-call | tf_op jit(solution)/shard_map/forward_all/pallas_call | solution.py:728
  99.1 148.8 %backward_all.1 = (f32[512,768]{1,0:T(8,128)}, bf16[9,256,768]{2,1,0:T(8,128)(2,1)}, bf16[144,768]{1,0:T(8,128)(2,1)}, f32[16,768]{1,0:T(8,128)}) custom-call(bf16[3,4,768,768]{3,2,1,0:T(8,128)(2,1)} %get-tuple-element.44.weights_in, f32[16,768]{1,0:T(8,128)} %reshape.60.refs_11_.vectors, s32[4,512]{1,0:T(4,128)} %boxes.1, s32[4,512]{1,0:T(4,128)} %segments.1, ...), custom_call_target="tpu_custom_call" | custom-call | tf_op jit(solution)/shard_map/backward_all/pallas_call | solution.py:1354
  247.9 1.4 slice.87
  249.2 1.6 fusion.2
  250.8 1.7 slice_reduce_fusion
  252.6 4.7 %fusion = (f32[3,256,768]{2,1,0:T(8,128)}, f32[3,256,768]{2,1,0:T(8,128)}, f32[3,256,768]{2,1,0:T(8,128)S(1)}) fusion(bf16[9,256,768]{2,1,0:T(8,128)(2,1)} %get-tuple-element.61), kind=kLoop, calls=%fused_computation.10 | loop fusion | bytes 14155776 | tf_op jit(solution)/shard_map/unstack | solution.py:1485
  257.2 0.0 copy-start
  257.2 1.4 fusion.1
  258.7 0.0 copy-start.1
  258.7 1.5 fusion.3
  260.1 0.0 copy-done
  260.1 1.1 copy.53
  261.3 0.0 copy-done.1
  261.3 1.1 copy.54
  (2 shorter events, 0.0 us)
Async XLA Ops:
  257.2 2.9 %copy-start = (f32[512,768]{1,0:T(8,128)S(1)}, f32[512,768]{1,0:T(8,128)}, u32[]{:S(2)}) copy-start(f32[512,768]{1,0:T(8,128)} %get-tuple-element.108) | copy-start | bytes 4718596
  258.7 2.6 copy-start.1

commit v4 on v2

--- a/solution.py
+++ b/solution.py
@@ -1334,7 +1334,10 @@
         seldom(vector_reduce(place, links, vector_terms, vector_land, vector_sems), 3),
     )
     table_sum[...] = slab_at(place.dp, place.half)[...]
-    vector_sum[...] = vector_terms[bits + 2]
+    vector_sum[0:16] = vector_terms[bits + 2]
+    vector_sum[16:17] = vector_terms[bits + 2, pl.ds(8 + t, 1)]
+    vector_sum[17:18] = vector_terms[bits + 2, pl.ds(12 + t, 1)]
+    vector_sum[18:24] = jnp.zeros((6, width), F32)
     word_copy.wait()
     links.finish()
     sums.finish(chunks)
@@ -1357,7 +1360,7 @@
             shape((tokens, width), F32),
             shape((chunks, part, width), BF16),
             shape((slab_rows, width), BF16),
-            shape((16, width), F32),
+            shape((24, width), F32),
         ],
         in_specs=[anywhere]
         + [in_vmem] * 6
@@ -1443,7 +1446,6 @@
     cotangent,
 ):
     own_rows, width = word_vectors.shape
-    t = lax.axis_index("tensor")
     owned = (position_table, horizontal_table, vertical_table, height_table, width_table)
     slab_rows = sum(table.shape[0] for table in owned)
     slab_padded = -(-slab_rows // 16) * 16
@@ -1487,8 +1489,7 @@
     first = [0]
     for own in owns:
         first.append(first[-1] + own)
-    bias_in = lax.dynamic_slice_in_dim(vector_sum, 8 + t, 1)[0]
-    bias_row = lax.dynamic_slice_in_dim(vector_sum, 12 + t, 1)[0]
+    bias_in, bias_row = vector_sum[16], vector_sum[17]
     bias_query, bias_value = bias_row[:fourth], bias_row[2 * fourth : 3 * fourth]
     return (
         layer_out,

time: 265 us -> 266 us (level)
  no operation moved by 1% of the time
where the time goes in v4:
time: 266 us; the launch traced here: 265 us
  Pallas kernels  248 us (93%)
  local copies, waits for them, and re-layouts  16.7 us (6%)
    pallas_call x1, Pallas kernels, backward_all(): pl.pallas_call(functools.partial(backward_kernel, bits, owns, slab_rows),...  148 us
    pallas_call x1, Pallas kernels, forward_all(): pl.pallas_call(functools.partial(forward_kernel, bits, owns, slab_rows, l...  99.4 us

profile of v4, /device:TPU:0, one launch (start us, length us, event | category | flops | bytes accessed | tf_op | source)
XLA Modules:
  0.0 265.1 jit_solution(6858640869281344369)
XLA Ops:
  0.7 0.9 concatenate.3
  1.6 0.6 reshape.60.refs_11_.vectors
  2.2 99.4 %forward_all.1 = (f32[512,768]{1,0:T(8,128)}, f32[512,768]{1,0:T(8,128)}, f32[8,768]{1,0:T(8,128)}, bf16[3,4,768,768]{3,2,1,0:T(8,128)(2,1)}, bf16[512,768]{1,0:...) custom-call(bf16[16,768]{1,0:T(8,128)(2,1)} %refs_0_.1, ...), custom_call_target="tpu_custom_call" | custom-call | tf_op jit(solution)/shard_map/forward_all/pallas_call | solution.py:728
  101.6 148.2 %backward_all.1 = (f32[512,768]{1,0:T(8,128)}, bf16[9,256,768]{2,1,0:T(8,128)(2,1)}, bf16[144,768]{1,0:T(8,128)(2,1)}, f32[24,768]{1,0:T(8,128)}) custom-call(bf16[3,4,768,768]{3,2,1,0:T(8,128)(2,1)} %get-tuple-element.44.weights_in, f32[16,768]{1,0:T(8,128)} %reshape.60.refs_11_.vectors, s32[4,512]{1,0:T(4,128)} %boxes.1, s32[4,512]{1,0:T(4,128)} %segments.1, ...), custom_call_target="tpu_custom_call" | custom-call | tf_op jit(solution)/shard_map/backward_all/pallas_call | solution.py:1357
  249.9 1.3 fusion.3
  251.1 1.7 slice_reduce_fusion
  252.9 1.4 slice.94
  254.2 1.6 fusion.2
  255.8 4.7 %fusion = (f32[3,256,768]{2,1,0:T(8,128)}, f32[3,256,768]{2,1,0:T(8,128)}, f32[3,256,768]{2,1,0:T(8,128)S(1)}) fusion(bf16[9,256,768]{2,1,0:T(8,128)(2,1)} %get-tuple-element.61), kind=kLoop, calls=%fused_computation.9 | loop fusion | bytes 14155776 | tf_op jit(solution)/shard_map/unstack | solution.py:1487
  260.5 0.0 copy-start
  260.5 1.4 fusion.1
  261.9 0.0 copy-start.1
  261.9 0.8 copy-done
  262.8 1.1 copy.53
  263.9 0.0 copy-done.1
  263.9 1.1 copy.54
  (2 shorter events, 0.0 us)
Async XLA Ops:
  260.5 2.3 copy-start
  261.9 2.0 copy-start.1
